TPU v7x, 256 devices: a whole 4x4x8 slice. The times are simulated.
256 devices in a mesh: dp: 8 (over x, y_hi), seq: 2 (over core), tensor: 16 (over z, y_lo).
Axes of the slice: x: 4, y: 4 (y_hi: 2, y_lo: 2; y = y_hi * 2 + y_lo), z: 8, core: 2. Of those that a mesh axis runs over, the one named last changes fastest.
Arguments:
- anchor: bfloat16 [8, 384, 8192], P('dp', 'seq'), may hold values from -42 to 42
- augment: bfloat16 [8, 384, 3584], P('dp', 'seq'), may hold values from -6 to 6
- lag: int32 [8], P('dp'), may hold values from 0 to 191
- w_query: bfloat16 [8192, 4096], P(('dp', 'seq'), 'tensor'), may hold values from -0.0625 to 0.0625
- w_key: bfloat16 [3584, 4096], P(('dp', 'seq'), 'tensor'), may hold values from -0.09375 to 0.09375
- w_value: bfloat16 [3584, 4096], P(('dp', 'seq'), 'tensor'), may hold values from -0.09375 to 0.09375
- w_out: bfloat16 [4096, 8192], P('tensor', ('dp', 'seq')), may hold values from -0.375 to 0.375
- cotangent: bfloat16 [8, 384, 8192], P('dp', 'seq', 'tensor'), may hold values from -6 to 6
Outputs:
- update: bfloat16 [8, 384, 8192], P('dp', 'seq', 'tensor')
- grad_query: bfloat16 [8192, 4096], P(('dp', 'seq'), 'tensor')
- grad_key: bfloat16 [3584, 4096], P(('dp', 'seq'), 'tensor')
- grad_value: bfloat16 [3584, 4096], P(('dp', 'seq'), 'tensor')
- grad_out: bfloat16 [4096, 8192], P('tensor', ('dp', 'seq'))
All inputs are finite; a program needn't handle non-finite values.
Results may differ from a plain program's by a relative error of at most 0.029.
The roundings to bfloat16 on the way count: a program that leaves them out, or rounds other values in their place, can miss the bound.
Values may be sent and summed in bfloat16 or wider, within the bound.
A program may use at most 128 MiB of HBM per device.

v0:
```python
import jax
import jax.numpy as jnp
from jax import lax
from jax.sharding import PartitionSpec as P

HEAD_DIM = 128


def gather_rows(left, piece):
    return jnp.dot(left, piece, preferred_element_type=jnp.float32)


def project_pair(source, w_key, w_value):
    keys = gather_rows(source, lax.all_gather(w_key, ("dp", "seq"), axis=0, tiled=True))
    values = gather_rows(source, lax.all_gather(w_value, ("dp", "seq"), axis=0, tiled=True))
    return (keys.astype(jnp.bfloat16), values.astype(jnp.bfloat16))


def contract_first(left, right):
    return lax.dot_general(
        left, right, (((0,), (0,)), ((), ())), preferred_element_type=jnp.float32
    )


def contract_second(left, right):
    return lax.dot_general(
        left, right, (((1,), (1,)), ((), ())), preferred_element_type=jnp.float32
    )


def local(anchor, augment, lag, w_query, w_key, w_value, w_out, cotangent):
    tok_rows = anchor.shape[1]
    source = anchor[0]
    states = augment[0]
    columns = w_query.shape[1]
    head_count = columns // HEAD_DIM
    factor = HEAD_DIM ** (-0.5)
    query = gather_rows(source, lax.all_gather(w_query, ("dp", "seq"), axis=0, tiled=True)).astype(
        jnp.bfloat16
    )
    states_all = lax.all_gather(states, "seq", axis=0, tiled=True)
    keys, values = project_pair(states_all, w_key, w_value)
    length = keys.shape[0]
    offset = lax.axis_index("seq") * tok_rows
    query_pos = lax.broadcasted_iota(jnp.int32, (tok_rows, length), 0) + offset + lag[0]
    key_pos = lax.broadcasted_iota(jnp.int32, (tok_rows, length), 1)
    allowed = key_pos <= query_pos
    query_heads = query.reshape(tok_rows, head_count, HEAD_DIM)
    key_heads = keys.reshape(length, head_count, HEAD_DIM)
    value_heads = values.reshape(length, head_count, HEAD_DIM)
    scores = (
        jnp.einsum("thd,shd->hts", query_heads, key_heads, preferred_element_type=jnp.float32)
        * factor
    )
    scores = jnp.where(allowed[None], scores, -jnp.inf)
    highest = jnp.max(scores, axis=2, keepdims=True)
    expo = jnp.exp(scores - highest)
    probs = expo / jnp.sum(expo, axis=2, keepdims=True)
    attention = probs.astype(jnp.bfloat16)
    context_heads = jnp.einsum(
        "hts,shd->thd", attention, value_heads, preferred_element_type=jnp.float32
    ).astype(jnp.bfloat16)
    context = context_heads.reshape(tok_rows, columns)
    out_full = lax.all_gather(w_out, ("dp", "seq"), axis=1, tiled=True)
    partial_update = jnp.dot(context, out_full, preferred_element_type=jnp.float32)
    update = lax.psum_scatter(
        partial_update[None].astype(jnp.bfloat16), "tensor", scatter_dimension=2, tiled=True
    )
    cotangent_full = lax.all_gather(cotangent, "tensor", axis=2, tiled=True)[0]
    back_context = contract_second(cotangent_full, out_full).astype(jnp.bfloat16)
    back_heads = back_context.reshape(tok_rows, head_count, HEAD_DIM)
    dprobs = jnp.einsum("thd,shd->hts", back_heads, value_heads, preferred_element_type=jnp.float32)
    delta = jnp.sum(
        back_heads.astype(jnp.float32) * context_heads.astype(jnp.float32), axis=2
    ).transpose(1, 0)
    dscores = (probs * (dprobs - delta[:, :, None]) * factor).astype(jnp.bfloat16)
    query_back = (
        jnp.einsum("hts,shd->thd", dscores, key_heads, preferred_element_type=jnp.float32)
        .astype(jnp.bfloat16)
        .reshape(tok_rows, columns)
    )
    key_terms = jnp.einsum(
        "hts,thd->shd", dscores, query_heads, preferred_element_type=jnp.float32
    ).reshape(length, columns)
    value_terms = jnp.einsum(
        "hts,thd->shd", attention, back_heads, preferred_element_type=jnp.float32
    ).reshape(length, columns)
    key_sum, value_sum = (
        lax.psum_scatter(key_terms, "seq", scatter_dimension=0, tiled=True),
        lax.psum_scatter(value_terms, "seq", scatter_dimension=0, tiled=True),
    )
    key_value_back = jnp.concatenate(
        [key_sum.astype(jnp.bfloat16), value_sum.astype(jnp.bfloat16)], axis=1
    )
    grad_query = lax.psum_scatter(
        contract_first(source, query_back).astype(jnp.bfloat16),
        ("dp", "seq"),
        scatter_dimension=0,
        tiled=True,
    )
    both_grads = lax.psum_scatter(
        contract_first(states, key_value_back).astype(jnp.bfloat16),
        ("dp", "seq"),
        scatter_dimension=0,
        tiled=True,
    )
    grad_key = both_grads[:, :columns]
    grad_value = both_grads[:, columns:]
    grad_out = lax.psum_scatter(
        contract_first(context, cotangent_full).astype(jnp.bfloat16),
        ("dp", "seq"),
        scatter_dimension=1,
        tiled=True,
    )
    return (update, grad_query, grad_key, grad_value, grad_out)


def solution(mesh):
    placed = (
        P("dp", "seq", None),
        P("dp", "seq", None),
        P("dp"),
        P(("dp", "seq"), "tensor"),
        P(("dp", "seq"), "tensor"),
        P(("dp", "seq"), "tensor"),
        P("tensor", ("dp", "seq")),
        P("dp", "seq", "tensor"),
    )
    return jax.shard_map(
        local,
        mesh=mesh,
        in_specs=placed,
        out_specs=(
            P("dp", "seq", "tensor"),
            P(("dp", "seq"), "tensor"),
            P(("dp", "seq"), "tensor"),
            P(("dp", "seq"), "tensor"),
            P("tensor", ("dp", "seq")),
        ),
        check_vma=False,
    )
```

profile of v0, /device:TPU:1, one launch (start us, length us, event | category | flops | bytes accessed | tf_op | source)
XLA Modules:
  0.0 746.8 jit_solution(9831117389074778509)
XLA Ops:
  7.2 0.7 all-gather.18.cloned.1.call-update
  8.0 0.7 all-gather.12.cloned.1.call-update
  8.7 0.7 all-gather.10.cloned.1.call-update
  9.4 0.5 all-gather.16.cloned.1.call-update
  10.0 0.5 all-gather.14.cloned.1.call-update
  10.6 0.5 all-gather.8.cloned.1.call-update
  11.8 0.1 iota_compare_fusion
  12.0 19.3 %all-gather.18.cloned.1.call-done = bf16[1,384,3584]{2,1,0:T(8,128)(2,1)} async-done(((bf16[1,192,3584]{2,1,0:T(8,128)(2,1)}), bf16[1,384,3584]{2,1,0:T(8,128)(2,1)}) %all-gather.18.cloned.1.call-update) | async-done | bytes 2752528 | tf_op jit(solution)/shard_map/all_gather | solution.py:41
  31.3 56.3 %all-gather.12.cloned.1.call-done = bf16[3584,256]{1,0:T(8,128)(2,1)} async-done(((bf16[224,256]{1,0:T(8,128)(2,1)}), bf16[3584,256]{1,0:T(8,128)(2,1)}) %all-gather.12.cloned.1.call-update) | async-done | bytes 1835024 | tf_op jit(solution)/shard_map/all_gather | solution.py:14
  87.5 3.5 fusion.24
  91.1 59.3 %all-gather.10.cloned.1.call-done = bf16[8192,256]{1,0:T(8,128)(2,1)} async-done(((bf16[512,256]{1,0:T(8,128)(2,1)}), bf16[8192,256]{1,0:T(8,128)(2,1)}) %all-gather.10.cloned.1.call-update) | async-done | bytes 4194320 | tf_op jit(solution)/shard_map/all_gather | solution.py:38
  150.4 3.2 fusion.36
  153.6 1.2 fusion.69
  154.8 1.2 fusion.43
  156.0 72.3 %all-gather.16.cloned.1.call-done = bf16[1,192,8192]{2,1,0:T(8,128)(2,1)} async-done(((bf16[1,192,512]{2,1,0:T(8,128)(2,1)}), bf16[1,192,8192]{2,1,0:T(8,128)(2,1)}) %all-gather.16.cloned.1.call-update) | async-done | bytes 3145744 | tf_op jit(solution)/shard_map/all_gather | solution.py:69
  228.3 69.5 %all-gather.14.cloned.1.call-done = bf16[256,8192]{1,0:T(8,128)(2,1)} async-done(((bf16[256,512]{1,0:T(8,128)(2,1)}), bf16[256,8192]{1,0:T(8,128)(2,1)}) %all-gather.14.cloned.1.call-update) | async-done | bytes 4194320 | tf_op jit(solution)/shard_map/all_gather | solution.py:64
  297.8 4.7 fusion.33
  302.4 1.0 fusion.48
  303.5 1.9 copy.56
  305.4 0.0 reduce-scatter.19.cloned.1.call-start
  305.5 46.2 %all-gather.8.cloned.1.call-done = bf16[3584,256]{1,0:T(8,128)(2,1)} async-done(((bf16[224,256]{1,0:T(8,128)(2,1)}), bf16[3584,256]{1,0:T(8,128)(2,1)}) %all-gather.8.cloned.1.call-update) | async-done | bytes 1835024 | tf_op jit(solution)/shard_map/all_gather | solution.py:15
  351.6 3.5 fusion.21
  355.2 0.9 multiply_reduce_fusion
  356.1 0.2 fusion.20
  356.4 0.7 copy-done.1
  357.1 1.2 fusion.51
  358.2 0.9 copy.54
  359.2 0.0 reduce-scatter.15.cloned.1.call-start
  359.2 1.3 fusion.39
  360.6 3.3 fusion.1
  363.8 0.0 reduce-scatter.23.cloned.1.call-start
  363.9 2.7 reduce-scatter.21.cloned.1.call-done
  366.6 1.0 copy.57
  367.6 16.1 %reduce-scatter.19.cloned.1.call-done = f32[192,256]{1,0:T(8,128)} async-done(((f32[384,256]{1,0:T(8,128)}), f32[192,256]{1,0:T(8,128)}) %reduce-scatter.19.cloned.1.call-update) | async-done | bytes 196624
  383.7 1.0 copy.55
  384.7 4.3 fusion.3
  389.0 5.9 copy.58
  394.9 0.0 reduce-scatter.13.cloned.1.call-start
  394.9 0.8 copy-done.2
  395.7 4.9 fusion.2
  400.6 0.0 reduce-scatter.17.cloned.1.call-start
  400.7 5.3 convolution_convert_fusion
  406.0 69.2 %reduce-scatter.15.cloned.1.call-done = bf16[512,256]{0,1:T(8,128)(2,1)} async-done(((bf16[8192,256]{0,1:T(8,128)(2,1)}), bf16[512,256]{0,1:T(8,128)(2,1)}) %reduce-scatter.15.cloned.1.call-update) | async-done | bytes 262160 | tf_op jit(solution)/shard_map/reduce_scatter | solution.py:95
  475.2 1.8 copy.47
  477.0 87.0 %reduce-scatter.23.cloned.1.call-done = bf16[224,512]{1,0:T(8,128)(2,1)} async-done(((bf16[3584,512]{1,0:T(8,128)(2,1)}), bf16[224,512]{1,0:T(8,128)(2,1)}) %reduce-scatter.23.cloned.1.call-update) | async-done | bytes 229392
  564.0 1.7 fusion.68
  565.7 79.5 %reduce-scatter.13.cloned.1.call-done = bf16[1,192,512]{2,1,0:T(8,128)(2,1)} async-done(((bf16[1,192,8192]{2,1,0:T(8,128)(2,1)}), bf16[1,192,512]{2,1,0:T(8,128)(2,1)}) %reduce-scatter.13.cloned.1.call-update) | async-done | bytes 196624 | tf_op jit(solution)/shard_map/reduce_scatter | solution.py:66
  645.2 94.8 %reduce-scatter.17.cloned.1.call-done = bf16[256,512]{1,0:T(8,128)(2,1)} async-done(((bf16[256,8192]{1,0:T(8,128)(2,1)}), bf16[256,512]{1,0:T(8,128)(2,1)}) %reduce-scatter.17.cloned.1.call-update) | async-done | bytes 262160 | tf_op jit(solution)/shard_map/reduce_scatter | solution.py:109
  (24 shorter events, 0.4 us)
Async XLA Ops:
  7.2 143.2 %copy-start = (bf16[1,192,8192]{2,1,0:T(8,128)(2,1)S(1)}, bf16[1,192,8192]{2,1,0:T(8,128)(2,1)}, u32[]{:S(2)}) copy-start(bf16[1,192,8192]{2,1,0:T(8,128)(2,1)} %param.8) | copy-start | bytes 9437188
  7.2 24.1 %all-gather.18.cloned.1.call-start = ((), (), s32[]{:S(2)}) async-start(), calls=%async_computation.14 | async-start | bytes 4128768 | tf_op jit(solution)/shard_map/all_gather | solution.py:41
  7.9 79.6 %all-gather.12.cloned.1.call-start = ((), (), s32[]{:S(2)}) async-start(), calls=%async_computation.8 | async-start | bytes 1949696 | tf_op jit(solution)/shard_map/all_gather | solution.py:14
  8.7 141.7 %all-gather.10.cloned.1.call-start = ((), (), s32[]{:S(2)}) async-start(), calls=%async_computation.7 | async-start | bytes 4456448 | tf_op jit(solution)/shard_map/all_gather | solution.py:38
  9.4 218.9 %all-gather.16.cloned.1.call-start = ((), (), s32[]{:S(2)}) async-start(), calls=%async_computation.11 | async-start | bytes 3342336 | tf_op jit(solution)/shard_map/all_gather | solution.py:69
  10.0 287.8 %all-gather.14.cloned.1.call-start = ((), (), s32[]{:S(2)}) async-start(), calls=%async_computation.9 | async-start | bytes 4456448 | tf_op jit(solution)/shard_map/all_gather | solution.py:64
  10.6 341.1 %all-gather.8.cloned.1.call-start = ((), (), s32[]{:S(2)}) async-start(), calls=%async_computation.6 | async-start | bytes 1949696 | tf_op jit(solution)/shard_map/all_gather | solution.py:15
  11.1 355.4 %reduce-scatter.21.cloned.1.call-start = ((), (), s32[]{:S(2)}) async-start(), calls=%async_computation.16 | async-start | bytes 589824
  91.0 62.5 %copy-start.5 = (bf16[384,256]{0,1:T(8,128)(2,1)}, bf16[384,256]{0,1:T(8,128)(2,1)S(1)}, u32[]{:S(2)}) copy-start(bf16[384,256]{0,1:T(8,128)(2,1)S(1)} %fusion.24) | copy-start | bytes 589828
  153.6 1.2 copy-start.4
  305.4 78.2 %reduce-scatter.19.cloned.1.call-start = ((), (), s32[]{:S(2)}) async-start(), calls=%async_computation.15 | async-start | bytes 589824
  351.6 4.5 copy-start.3
  356.4 0.7 copy-start.1
  359.2 116.0 %reduce-scatter.15.cloned.1.call-start = ((), (), s32[]{:S(2)}) async-start(), calls=%async_computation.12 | async-start | bytes 4456448 | tf_op jit(solution)/shard_map/reduce_scatter | solution.py:95
  363.8 200.2 %reduce-scatter.23.cloned.1.call-start = ((), (), s32[]{:S(2)}) async-start(), calls=%async_computation.17 | async-start | bytes 3899392
  394.8 0.9 copy-start.2
  394.9 250.3 %reduce-scatter.13.cloned.1.call-start = ((), (), s32[]{:S(2)}) async-start(), calls=%async_computation.10 | async-start | bytes 3342336 | tf_op jit(solution)/shard_map/reduce_scatter | solution.py:66
  400.6 339.4 %reduce-scatter.17.cloned.1.call-start = ((), (), s32[]{:S(2)}) async-start(), calls=%async_computation.13 | async-start | bytes 4456448 | tf_op jit(solution)/shard_map/reduce_scatter | solution.py:109
Sparse Core Ops, SparseCore 0:
  9.8 21.3 all-gather.17
  33.9 53.5 all-gather.11
  90.2 60.0 all-gather.9
  152.0 76.2 all-gather.15
  230.7 67.0 all-gather.13
  300.3 51.2 all-gather.7
  354.1 12.3 reduce-scatter.20
  369.2 14.3 reduce-scatter.18
  388.0 87.1 reduce-scatter.14
  480.0 83.9 reduce-scatter.22
  567.3 77.7 reduce-scatter.12
  650.6 89.3 reduce-scatter.16
where the time goes:
time: 748 us; the launch traced here: 747 us
  waiting for transfers between devices  676 us (90%)
  matrix products  38.5 us (5%)
  local copies, waits for them, and re-layouts  15.7 us (2%)
  between operations  15 us (2%)
    unnamed x15, waiting for transfers between devices  109 us
    reduce_scatter x1, waiting for transfers between devices, local(): lax.psum_scatter(contract_first(context, cotangent_full).astype(jnp.bfloa...  94.8 us
    reduce_scatter x1, waiting for transfers between devices, local(): lax.psum_scatter(partial_update[None].astype(jnp.bfloat16), 'tensor', sca...  79.5 us
    all_gather x1, waiting for transfers between devices, local(): cotangent_full = lax.all_gather(cotangent, 'tensor', axis=2, tiled=True)[0]  72.3 us
    all_gather x1, waiting for transfers between devices, local(): out_full = lax.all_gather(w_out, ('dp', 'seq'), axis=1, tiled=True)  69.5 us
    reduce_scatter x1, waiting for transfers between devices, local(): lax.psum_scatter(contract_first(source, query_back).astype(jnp.bfloat16),...  69.2 us
    all_gather x1, waiting for transfers between devices, local(): lax.all_gather(w_query, ('dp', 'seq'), axis=0, tiled=True)  59.3 us
    all_gather x1, waiting for transfers between devices, project_pair(): lax.all_gather(w_key, ('dp', 'seq'), axis=0, tiled=True)  56.3 us
  transfers between devices with their start and end apart: 12, of which 12 were waited for; matrix products, arithmetic and copies ran while one was open for 7% of the time, Pallas kernels for 0%

commit v1 on v0

v1 whole, which is shorter than its diff:
```python
import functools

import jax
import jax.numpy as jnp
from jax import lax
from jax.experimental import pallas as pl
from jax.experimental.pallas import tpu as pltpu
from jax.sharding import PartitionSpec as P

MESH = pl.DeviceIdType.MESH
BF = jnp.bfloat16
F32 = jnp.float32
HEAD = 128
TOK = 192
LEN = 384
NS = 8
COPIES = 128


def nn(a, b):
    return jnp.dot(a, b, preferred_element_type=F32)


def nt(a, b):
    return lax.dot_general(a, b, (((1,), (1,)), ((), ())), preferred_element_type=F32)


def tn(a, b):
    return lax.dot_general(a, b, (((0,), (0,)), ((), ())), preferred_element_type=F32)


def kernel(
    anchor, augment, lag, w_query, w_key, w_value, w_out, cot_in,
    update, g_query, g_key, g_value, g_out,
    anc, anc_t, sts, sts_t, cot, wq, wkv, wo,
    s_out, s_kv, s_q, upd, rz, ru,
    ra_out, rc_out, ry_out, ra_kv, rc_kv, ry_kv, ra_q, rc_q, ry_q,
    part, part_kv, other, other_kv, q_h, k_h, v_h, b_h, probs, att, ctx, qb, kvb,
    send, recv, near_send, near_recv, fin_recv, local,
):
    dp, c, t = lax.axis_index("dp"), lax.axis_index("seq"), lax.axis_index("tensor")
    z, yl = t // 2, t % 2
    o = 1 - c
    xr, xl = (dp + 2) % NS, (dp + 6) % NS
    yp = dp + 1 - 2 * (dp % 2)
    tn_ = t + 1 - 2 * yl
    to_xr, to_xl, to_yp = (xr, c, t), (xl, c, t), (yp, c, t)
    to_zr, to_zl = (dp, c, (t + 2) % 16), (dp, c, (t + 14) % 16)
    to_sib = (dp, o, t)
    same = c == yl

    barrier = pltpu.get_barrier_semaphore()
    partners = (to_xr, to_xl, to_yp, to_zr, to_zl, to_sib, (dp, 0, tn_), (dp, 1, tn_))
    for who in partners:
        pl.semaphore_signal(barrier, inc=1, device_id=who, device_id_type=MESH)
    pl.semaphore_wait(barrier, len(partners))

    started = []

    def push(src, dst, who):
        i = len(started)
        copy = pltpu.make_async_remote_copy(
            src_ref=src, dst_ref=dst, send_sem=send.at[i], recv_sem=recv.at[i],
            device_id=who, device_id_type=MESH,
        )
        copy.start()
        started.append(copy)
        return copy

    locals_ = []

    def fetch(src, dst):
        copy = pltpu.make_async_copy(src, dst, local.at[len(locals_)])
        copy.start()
        locals_.append(copy)
        return copy

    def col(i, n):
        return pl.ds(pl.multiple_of(i * n, n), n)

    mine = pl.ds(pl.multiple_of(c * TOK, TOK), TOK)
    head = col(c, HEAD)
    head_o = col(o, HEAD)

    def kv_rows(k, half):
        base = (2 * k + c) * 224
        if half is None:
            return pl.ds(pl.multiple_of(base, 224), 224)
        return pl.ds(pl.multiple_of(base + half * 112, 112), 112)

    def slot_k(k, half=None):
        return wkv.at[kv_rows(k, half), pl.ds(0, 256)]

    def slot_v(k, half=None):
        return wkv.at[kv_rows(k, half), pl.ds(256, 256)]

    def slot_q(k, half=None):
        return wq.at[k] if half is None else wq.at[k, pl.ds(half * 256, 256)]

    def slot_o(k, half=None):
        return wo.at[k] if half is None else wo.at[k, pl.ds(half * 128, 128)]

    def flip(k):
        return k + 1 - 2 * (k % 2)

    class YFirst:
        def __init__(self, src, slot):
            self.slot = slot
            self.own = [push(src, slot(dp), w) for w in (to_xr, to_xl, to_yp)]
            fetch(src, slot(dp))

        def from_y(self):
            self.own[2].wait_recv()
            s = self.slot(yp)
            self.far = [push(s, s, to_xr), push(s, s, to_xl)]

        def from_x(self):
            self.own[0].wait_recv()
            self.own[1].wait_recv()
            a, b = self.slot(xl, 0), self.slot(xr, 1)
            self.halves = [push(a, a, to_xr), push(b, b, to_xl)]

        def from_x_far(self):
            self.far[0].wait_recv()
            self.far[1].wait_recv()
            a, b = self.slot(flip(xl), 0), self.slot(flip(xr), 1)
            self.halves += [push(a, a, to_xr), push(b, b, to_xl)]

        def finish(self):
            for copy in self.halves:
                copy.wait_recv()

    class XFirst:
        def __init__(self, src, slot):
            self.slot = slot
            self.own = [push(src, slot(dp), w) for w in (to_yp, to_xr, to_xl)]
            fetch(src, slot(dp))

        def from_x(self):
            self.own[1].wait_recv()
            self.own[2].wait_recv()
            a, b = self.slot(xl, 0), self.slot(xr, 1)
            self.halves = [push(a, a, to_xr), push(b, b, to_xl)]
            a, b = self.slot(xl), self.slot(xr)
            self.last = [self.own[0], push(a, a, to_yp), push(b, b, to_yp)]

        def from_x_far(self):
            far = (dp + 4) % NS
            for half in (0, 1):
                self.halves[half].wait_recv()
                s = self.slot(far, half)
                self.last.append(push(s, s, to_yp))

        def finish(self):
            for copy in self.last:
                copy.wait_recv()

    ag_k = YFirst(w_key, slot_k)
    ag_v = YFirst(w_value, slot_v)

    cot_dst = cot.at[z, mine]
    cot_far = pltpu.make_async_remote_copy(
        src_ref=cot_in.at[0], dst_ref=cot_dst, send_sem=near_send.at[0], recv_sem=near_recv.at[c],
        device_id=(dp, yl, tn_), device_id_type=MESH)
    cot_sib = pltpu.make_async_remote_copy(
        src_ref=cot_in.at[0], dst_ref=cot_dst, send_sem=near_send.at[1], recv_sem=near_recv.at[c],
        device_id=to_sib, device_id_type=MESH)
    cot_own = pltpu.make_async_copy(cot_in.at[0], cot_dst, near_recv.at[c])
    cot_far.start()

    @pl.when(same)
    def _():
        cot_own.start()

    @pl.when(jnp.logical_not(same))
    def _():
        cot_sib.start()

    ag_q = YFirst(w_query, slot_q)
    ag_o = XFirst(w_out, slot_o)

    sib = [push(augment.at[0], sts.at[mine], to_sib)]
    fetch(augment.at[0], sts.at[mine])
    for k in range(NS):
        sib.append(push(anchor.at[0, :, pl.ds(pl.multiple_of((2 * k + o) * 512, 512), 512)], anc.at[k, mine], to_sib))
        fetch(anchor.at[0, :, pl.ds(pl.multiple_of((2 * k + c) * 512, 512), 512)], anc.at[k, mine])

    zero = jnp.zeros((224, 512), BF)
    for k in range(NS):
        wkv[pl.ds(pl.multiple_of((2 * k + o) * 224, 224), 224), :] = zero

    for h in (0, 1):
        pltpu.make_async_copy(cot.at[z, pl.ds(h * TOK, TOK)], cot.at[z, pl.ds(h * TOK, TOK)], near_recv.at[h]).wait()
    ring = []

    def ring_step(s):
        if s > 1:
            for copy in ring[-1]:
                copy.wait_recv()
        if s < 4:
            a, b = cot.at[(z + 9 - s) % NS], cot.at[(z + s - 1) % NS]
        else:
            a, b = cot.at[(z + 5) % NS, pl.ds(0, TOK)], cot.at[(z + 3) % NS, pl.ds(TOK, TOK)]
        ring.append([push(a, a, to_zr), push(b, b, to_zl)])

    ring_step(1)
    ag_k.from_y()
    ag_k.from_x()
    ag_v.from_y()
    ag_v.from_x()

    for copy in sib:
        copy.wait_recv()
    for copy in locals_:
        copy.wait()

    def turn_sts(j, _):
        sts_t[col(j, 512), :] = sts[:, col(j, 512)].T
        return _

    def turn_anc(k, _):
        anc_t[k] = anc[k].T
        return _

    lax.fori_loop(0, 7, turn_sts, 0)
    ring_step(2)
    ag_q.from_y()
    ag_q.from_x()
    lax.fori_loop(0, NS, turn_anc, 0)
    ag_o.from_x()
    ring_step(3)
    ag_k.from_x_far()
    ag_v.from_x_far()
    ag_q.from_x_far()
    ag_o.from_x_far()
    ag_k.finish()
    ag_v.finish()
    ring_step(4)

    part_kv[...] = nn(sts[:, pl.ds(0, 512)], wkv[pl.ds(0, 512), :])

    def add_kv(j, _):
        part_kv[...] += nn(sts[:, col(j, 512)], wkv[col(j, 512), :])
        return _

    lax.fori_loop(1, 7, add_kv, 0)
    ex_k = push(part_kv.at[:, head_o], other_kv.at[0], to_sib)
    ex_v = push(part_kv.at[:, pl.ds(pl.multiple_of(256 + o * HEAD, HEAD), HEAD)], other_kv.at[1], to_sib)
    ag_q.finish()
    part[0] = nn(anc[0], wq[0])

    def add_q(k, _):
        part[0] += nn(anc[k], wq[k])
        return _

    lax.fori_loop(1, NS, add_q, 0)
    ex_q = push(part.at[0, :, head_o], other.at[0], to_sib)
    ex_k.wait_recv()
    k_h[...] = (part_kv[:, head] + other_kv[0]).astype(BF)
    ex_v.wait_recv()
    v_h[...] = (part_kv[:, pl.ds(pl.multiple_of(256 + c * HEAD, HEAD), HEAD)] + other_kv[1]).astype(BF)
    ex_q.wait_recv()
    q_h[...] = (part[0, :, head] + other[0]).astype(BF)

    factor = HEAD ** (-0.5)
    step = 128
    for r in range(LEN // step):
        rows = pl.ds(r * step, step)
        scores = nt(q_h[rows, :], k_h[...]) * factor
        reach = lax.broadcasted_iota(jnp.int32, (step, LEN), 0) + (r * step + lag[0])
        allowed = lax.broadcasted_iota(jnp.int32, (step, LEN), 1) <= reach
        scores = jnp.where(allowed, scores, -jnp.inf)
        expo = jnp.exp(scores - jnp.max(scores, axis=1, keepdims=True))
        p = expo / jnp.sum(expo, axis=1, keepdims=True)
        probs[rows, :] = p
        a = p.astype(BF)
        att[rows, :] = a
        ctx[rows, head] = nn(a, v_h[...]).astype(BF)
    ex_ctx = push(ctx.at[:, head], ctx.at[:, head], to_sib)

    ag_o.finish()
    for copy in ring[-1]:
        copy.wait_recv()
    part[1] = nt(cot[0], wo[0])

    def add_b(k, _):
        part[1] += nt(cot[k], wo[k])
        return _

    lax.fori_loop(1, NS, add_b, 0)
    ex_b = push(part.at[1, :, head_o], other.at[1], to_sib)
    ex_ctx.wait_recv()

    def slot(off, j):
        k = (dp + 2 * off + NS) % NS
        return flip(k) if j else k

    class XFirstSum:
        def __init__(self, s, ra, rc, ry, make, out):
            self.s, self.ra, self.rc, self.ry, self.out = s, ra, rc, ry, out
            n = s.shape[1] // 2
            self.lo, self.hi = pl.ds(0, n), pl.ds(n, n)
            lo, hi = self.lo, self.hi
            self.a, self.b = [], []
            for j in (0, 1):
                k = slot(2, j)
                make(k)
                self.a += [push(s.at[k, lo], ra.at[0, j], to_xr), push(s.at[k, hi], ra.at[1, j], to_xl)]
            for j in (0, 1):
                k, m = slot(1, j), slot(-1, j)
                make(k)
                self.b.append(push(s.at[k, hi], rc.at[0, j, hi], to_xr))
                make(m)
                self.b.append(push(s.at[m, lo], rc.at[1, j, lo], to_xl))
            for j in (1, 0):
                make(slot(0, j))

        def pass_on(self):
            s, ra, rc = self.s, self.ra, self.rc
            for j in (0, 1):
                k, m = slot(1, j), slot(-1, j)
                self.a[2 * j].wait_recv()
                s[k, self.lo] = (s[k, self.lo].astype(F32) + ra[0, j].astype(F32)).astype(BF)
                self.b.append(push(s.at[k, self.lo], rc.at[0, j, self.lo], to_xr))
                self.a[2 * j + 1].wait_recv()
                s[m, self.hi] = (s[m, self.hi].astype(F32) + ra[1, j].astype(F32)).astype(BF)
                self.b.append(push(s.at[m, self.hi], rc.at[1, j, self.hi], to_xl))

        def total(self, j):
            k = slot(0, j)
            return self.s[k].astype(F32) + self.rc[0, j].astype(F32) + self.rc[1, j].astype(F32)

        def across(self):
            for copy in self.b:
                copy.wait_recv()
            k = slot(0, 1)
            self.s[k] = self.total(1).astype(BF)
            self.y = push(self.s.at[k], self.ry, to_yp)

        def finish(self):
            self.y.wait_recv()
            self.out(self.total(0) + self.ry[...].astype(F32))

    class YFirstSum:
        def __init__(self, s, ra, rc, ry, make, out):
            self.s, self.ra, self.rc, self.ry, self.out = s, ra, rc, ry, out
            n = s.shape[1] // 2
            self.lo, self.hi = pl.ds(0, n), pl.ds(n, n)
            self.y = []
            for i, off in enumerate((2, 1, -1, 0)):
                k = slot(off, 1)
                make(k)
                self.y.append(push(s.at[k], ry.at[i], to_yp))
            for off in (2, 1, -1, 0):
                make(slot(off, 0))

        def add(self, k, rows, got):
            self.s[k, rows] = (self.s[k, rows].astype(F32) + got.astype(F32)).astype(BF)

        def from_y(self):
            s, ra, rc, ry, lo, hi = self.s, self.ra, self.rc, self.ry, self.lo, self.hi
            self.y[0].wait_recv()
            k = slot(2, 0)
            s[k] = (s[k].astype(F32) + ry[0].astype(F32)).astype(BF)
            self.a = [push(s.at[k, lo], ra.at[0], to_xr), push(s.at[k, hi], ra.at[1], to_xl)]

        def from_y_near(self):
            s, rc, ry, lo, hi = self.s, self.rc, self.ry, self.lo, self.hi
            k, m = slot(1, 0), slot(-1, 0)
            self.y[1].wait_recv()
            s[k] = (s[k].astype(F32) + ry[1].astype(F32)).astype(BF)
            self.b = [push(s.at[k, hi], rc.at[0, hi], to_xr)]
            self.y[2].wait_recv()
            s[m] = (s[m].astype(F32) + ry[2].astype(F32)).astype(BF)
            self.b.append(push(s.at[m, lo], rc.at[1, lo], to_xl))

        def pass_on(self):
            k, m = slot(1, 0), slot(-1, 0)
            self.a[0].wait_recv()
            self.add(k, self.lo, self.ra[0])
            self.b.append(push(self.s.at[k, self.lo], self.rc.at[0, self.lo], to_xr))
            self.a[1].wait_recv()
            self.add(m, self.hi, self.ra[1])
            self.b.append(push(self.s.at[m, self.hi], self.rc.at[1, self.hi], to_xl))

        def finish(self):
            self.y[3].wait_recv()
            for copy in self.b:
                copy.wait_recv()
            k = slot(0, 0)
            self.out(self.s[k].astype(F32) + self.ry[3].astype(F32)
                     + self.rc[0].astype(F32) + self.rc[1].astype(F32))

    def make_out(k):
        s_out[k] = tn(ctx[...], cot[k]).astype(BF)

    def put_out(total):
        g_out[...] = total.astype(BF)

    rs_out = XFirstSum(s_out, ra_out, rc_out, ry_out, make_out, put_out)

    def make_upd(k, _):
        upd[k] = nn(ctx[...], wo[k]).astype(BF)
        return _

    lax.fori_loop(0, NS, make_upd, 0)
    zsum = []

    def z_step(s):
        if s == 1:
            far = (z + 4) % NS
            a, b = upd.at[far, pl.ds(0, TOK)], upd.at[far, pl.ds(TOK, TOK)]
            da, db = rz.at[0, 0, pl.ds(0, TOK)], rz.at[1, 0, pl.ds(TOK, TOK)]
        else:
            for copy in zsum[-1]:
                copy.wait_recv()
            k, m = (z + 5 - s) % NS, (z + 3 + s) % NS
            rows_k, rows_m = (pl.ds(0, TOK), pl.ds(TOK, TOK)) if s == 2 else (pl.ds(0, LEN), pl.ds(0, LEN))
            upd[k, rows_k] = (upd[k, rows_k].astype(F32) + rz[0, s - 2, rows_k].astype(F32)).astype(BF)
            upd[m, rows_m] = (upd[m, rows_m].astype(F32) + rz[1, s - 2, rows_m].astype(F32)).astype(BF)
            a, b = upd.at[k], upd.at[m]
            da, db = rz.at[0, s - 1], rz.at[1, s - 1]
        zsum.append([push(a, da, to_zr), push(b, db, to_zl)])

    z_step(1)

    ex_b.wait_recv()
    b_h[...] = (part[1, :, head] + other[1]).astype(BF)
    for r in range(LEN // step):
        rows = pl.ds(r * step, step)
        dprobs = nt(b_h[rows, :], v_h[...])
        delta = jnp.sum(b_h[rows, :].astype(F32) * ctx[rows, head].astype(F32), axis=1, keepdims=True)
        ds = (probs[rows, :] * (dprobs - delta) * factor).astype(BF)
        qb[rows, head] = nn(ds, k_h[...]).astype(BF)
        kt = tn(ds, q_h[rows, :])
        vt = tn(att[rows, :], b_h[rows, :])
        if r == 0:
            other_kv[0] = kt
            other_kv[1] = vt
        else:
            other_kv[0] += kt
            other_kv[1] += vt
    head_v = pl.ds(pl.multiple_of(256 + c * HEAD, HEAD), HEAD)
    kvb[:, head] = other_kv[0].astype(BF)
    kvb[:, head_v] = other_kv[1].astype(BF)
    ex_kb = push(kvb.at[:, head], kvb.at[:, head], to_sib)
    ex_vb = push(kvb.at[:, head_v], kvb.at[:, head_v], to_sib)
    ex_qb = push(qb.at[:, head], qb.at[:, head], to_sib)
    rs_out.pass_on()
    z_step(2)

    def make_kv(k):
        s_kv[k] = nn(sts_t[pl.ds(pl.multiple_of((2 * k + c) * 224, 224), 224), :], kvb[...]).astype(BF)

    def put_kv(total):
        g_key[...] = total[:, :256].astype(BF)
        g_value[...] = total[:, 256:].astype(BF)

    def make_q(k):
        s_q[k] = nn(anc_t[k], qb[...]).astype(BF)

    def put_q(total):
        g_query[...] = total.astype(BF)

    ex_qb.wait_recv()
    rs_q = YFirstSum(s_q, ra_q, rc_q, ry_q, make_q, put_q)
    ex_kb.wait_recv()
    ex_vb.wait_recv()
    rs_kv = XFirstSum(s_kv, ra_kv, rc_kv, ry_kv, make_kv, put_kv)

    rs_q.from_y()
    z_step(3)
    rs_out.across()
    rs_q.from_y_near()
    rs_kv.pass_on()
    z_step(4)
    rs_q.pass_on()
    rs_kv.across()
    rs_out.finish()

    for copy in zsum[-1]:
        copy.wait_recv()
    upd[z] = (upd[z].astype(F32) + rz[0, 3].astype(F32) + rz[1, 3].astype(F32)).astype(BF)
    kept = upd.at[z, mine]
    given = upd.at[z, pl.ds(pl.multiple_of(o * TOK, TOK), TOK)]
    fin_own = pltpu.make_async_copy(kept, ru.at[0], fin_recv.at[0])
    fin_sib = pltpu.make_async_remote_copy(
        src_ref=given, dst_ref=ru.at[0], send_sem=near_send.at[2], recv_sem=fin_recv.at[0],
        device_id=to_sib, device_id_type=MESH)
    fin_far = [
        pltpu.make_async_remote_copy(
            src_ref=upd.at[z, pl.ds(h * TOK, TOK)], dst_ref=ru.at[1], send_sem=near_send.at[3 + h],
            recv_sem=fin_recv.at[1], device_id=(dp, h, tn_), device_id_type=MESH)
        for h in (0, 1)
    ]

    @pl.when(same)
    def _():
        fin_own.start()
        fin_sib.start()

    @pl.when(jnp.logical_not(same))
    def _():
        fin_far[0].start()
        fin_far[1].start()

    rs_kv.finish()
    rs_q.finish()
    for i in (0, 1):
        pltpu.make_async_copy(ru.at[i], ru.at[i], fin_recv.at[i]).wait()
    update[0] = (ru[0].astype(F32) + ru[1].astype(F32)).astype(BF)

    for copy in started:
        copy.wait_send()
    cot_far.wait_send()

    @pl.when(jnp.logical_not(same))
    def _():
        cot_sib.wait_send()
        fin_far[0].wait_send()
        fin_far[1].wait_send()

    @pl.when(same)
    def _():
        fin_sib.wait_send()


def local(*args):
    vm = pltpu.VMEM
    shapes = [
        ((1, TOK, 512), BF), ((512, 256), BF), ((224, 256), BF), ((224, 256), BF), ((256, 512), BF),
    ]
    scratch = [
        vm((NS, LEN, 512), BF), vm((NS, 512, LEN), BF), vm((LEN, 3584), BF), vm((3584, LEN), BF),
        vm((NS, LEN, 512), BF), vm((NS, 512, 256), BF), vm((3584, 512), BF), vm((NS, 256, 512), BF),
        vm((NS, 256, 512), BF), vm((NS, 224, 512), BF), vm((NS, 512, 256), BF),
        vm((NS, LEN, 512), BF), vm((2, 4, LEN, 512), BF), vm((2, TOK, 512), BF),
        vm((2, 2, 128, 512), BF), vm((2, 2, 256, 512), BF), vm((256, 512), BF),
        vm((2, 2, 112, 512), BF), vm((2, 2, 224, 512), BF), vm((224, 512), BF),
        vm((2, 256, 256), BF), vm((2, 512, 256), BF), vm((4, 512, 256), BF),
        vm((2, LEN, 256), F32), vm((LEN, 512), F32), vm((2, LEN, HEAD), F32), vm((2, LEN, HEAD), F32),
        vm((LEN, HEAD), BF), vm((LEN, HEAD), BF), vm((LEN, HEAD), BF), vm((LEN, HEAD), BF),
        vm((LEN, LEN), F32), vm((LEN, LEN), BF), vm((LEN, 256), BF), vm((LEN, 256), BF), vm((LEN, 512), BF),
        pltpu.SemaphoreType.DMA((COPIES,)), pltpu.SemaphoreType.DMA((COPIES,)),
        pltpu.SemaphoreType.DMA((5,)), pltpu.SemaphoreType.DMA((2,)), pltpu.SemaphoreType.DMA((2,)),
        pltpu.SemaphoreType.DMA((16,)),
    ]
    any_ = pl.BlockSpec(memory_space=pl.ANY)
    return pl.pallas_call(
        kernel,
        out_shape=[jax.ShapeDtypeStruct(s, d) for s, d in shapes],
        in_specs=[any_, any_, pl.BlockSpec(memory_space=pltpu.SMEM)] + [any_] * 5,
        out_specs=[pl.BlockSpec(memory_space=pltpu.VMEM)] * 5,
        scratch_shapes=scratch,
        compiler_params=pltpu.CompilerParams(
            collective_id=0, has_side_effects=True, vmem_limit_bytes=58 * 2**20
        ),
        name="block",
    )(*args)


def solution(mesh):
    placed = (
        P("dp", "seq", None),
        P("dp", "seq", None),
        P("dp"),
        P(("dp", "seq"), "tensor"),
        P(("dp", "seq"), "tensor"),
        P(("dp", "seq"), "tensor"),
        P("tensor", ("dp", "seq")),
        P("dp", "seq", "tensor"),
    )
    return jax.shard_map(
        local,
        mesh=mesh,
        in_specs=placed,
        out_specs=(
            P("dp", "seq", "tensor"),
            P(("dp", "seq"), "tensor"),
            P(("dp", "seq"), "tensor"),
            P(("dp", "seq"), "tensor"),
            P("tensor", ("dp", "seq")),
        ),
        check_vma=False,
    )
```

time: 748 us -> 123 us (0.16)
  waiting for transfers between devices: 676 us -> 0 us
  Pallas kernels: 0 us -> 114 us
  matrix products: 38.5 us -> 0 us
  between operations: 15 us -> 1.29 us
  local copies, waits for them, and re-layouts: 15.7 us -> 8.05 us
    all_gather x6 -> x0, waiting for transfers between devices: 323 us -> none  [the longest x1 72.3 us: local(): cotangent_full = lax.all_gather(cotangent, 'tensor', axis=2, tiled=True)[0]]
    reduce_scatter x3 -> x0, waiting for transfers between devices: 244 us -> none  [the longest x1 94.8 us: local(): lax.psum_scatter(contract_first(context, cotangent_full).astype(jnp.bfloa...]
    pallas_call x0 -> x1, Pallas kernels: none -> 114 us  [local(): pl.pallas_call(kernel, out_shape=[jax.ShapeDtypeStruct(s, d) for s, d in...]
    unnamed x15 -> x0, waiting for transfers between devices: 109 us -> none
    dot_general x13 -> x0, matrix products: 37.3 us -> none  [the longest x3 12.9 us: contract_first(): lax.dot_general(left, right, (((0,), (0,)), ((), ())), preferred_element_...]
  transfers between devices with their start and end apart: 12 -> 0, of which waited for: 12 -> 0; matrix products, arithmetic and copies ran while one was open for 7% -> 0% of each run, Pallas kernels for 0% -> 0%
where the time goes in v1:
time: 123 us
  Pallas kernels  114 us (93%)
  local copies, waits for them, and re-layouts  8.05 us (7%)
  between operations  1.29 us (1%)
    pallas_call x1, Pallas kernels, local(): pl.pallas_call(kernel, out_shape=[jax.ShapeDtypeStruct(s, d) for s, d in...  114 us
    unnamed x5, local copies, waits for them, and re-layouts  8.05 us

profile of v1, /device:TPU:1, one launch (start us, length us, event | category | flops | bytes accessed | tf_op | source)
XLA Modules:
  0.0 122.9 jit_solution(12966178844157670766)
XLA Ops:
  1.3 113.5 %block.1 = (bf16[1,192,512]{2,1,0:T(8,128)(2,1)}, bf16[512,256]{1,0:T(8,128)(2,1)}, bf16[224,256]{1,0:T(8,128)(2,1)}, bf16[224,256]{1,0:T(8,128)(2,1)}, bf16[256,512]{1,0:T(8,128)(2,1)}) custom-call(bf16[1,192,8192]{2,1,0:T(8,128)(2,1)} %anchor.1, bf16[1,192,3584]{2,1,0:T(8,128)(2,1)} %augment.1, s32[1]{0:T(128)S(6)} %copy.18.lag, bf16[512,256]{1,0:T(8,128)(2,1)} %w_query.1, ...), custom_call_target="tpu_custom_call" | custom-call | tf_op jit(solution)/shard_map/block/pallas_call | solution.py:549
  114.8 1.6 %copy.19 = bf16[1,192,512]{2,1,0:T(8,128)(2,1)} copy(bf16[1,192,512]{2,1,0:T(8,128)(2,1)} %get-tuple-element.10) | data formatting | bytes 393216
  116.4 1.7 %copy.20 = bf16[512,256]{1,0:T(8,128)(2,1)} copy(bf16[512,256]{1,0:T(8,128)(2,1)} %get-tuple-element.11) | data formatting | bytes 524288
  118.1 1.6 %copy.21 = bf16[224,256]{1,0:T(8,128)(2,1)} copy(bf16[224,256]{1,0:T(8,128)(2,1)} %get-tuple-element.12) | data formatting | bytes 229376
  119.6 1.6 %copy.22 = bf16[224,256]{1,0:T(8,128)(2,1)} copy(bf16[224,256]{1,0:T(8,128)(2,1)} %get-tuple-element.13) | data formatting | bytes 229376
  121.2 1.7 %copy.23 = bf16[256,512]{1,0:T(8,128)(2,1)} copy(bf16[256,512]{1,0:T(8,128)(2,1)} %get-tuple-element.14) | data formatting | bytes 524288

commit v2 on v0

v2 whole, which is shorter than its diff:
```python
import jax
import jax.numpy as jnp
from jax import lax
from jax.experimental import pallas as pl
from jax.experimental.pallas import tpu as pltpu
from jax.sharding import PartitionSpec as P

MESH = pl.DeviceIdType.MESH
BF = jnp.bfloat16
F32 = jnp.float32
HEAD = 128
TOK = 192
LEN = 384
NS = 8
COPIES = 256

Q_Y, O_Y, GQ_Y, GO_Y = 384, 128, 320, 128

ORDER = (
    "z1a", "z1b", "kv.fx", "kv.fy", "qA.fx", "qB.fx", "z2a", "turn0", "turn1", "turn2", "turn3", "turn4",
    "qB.fy", "turn5", "z2b", "turn6", "turn7", "kv.fxf", "z3a", "qA.fxf", "own_o", "qB.fxf", "z3b", "kv",
    "oA.fx", "z4a", "oB.fx", "q", "oA.fxf", "oB.fy", "attn0", "attn1", "attn2", "oB.fxf", "goA.y0", "goA.y1",
    "goA.y2", "goA.y3", "goB.a0", "goB.a1", "goB.b0", "goB.b1", "goA.m", "goB.m0", "bc", "upd", "goB.p0",
    "goA.a", "goB.p1", "bwd0", "bwd1", "goA.b", "bwd2", "u2a", "goA.b_", "goA.p", "goA.p_", "goB.y", "gkv.a0",
    "gkv.a1", "gkv.b0", "gkv.b1", "u3b", "gqA.y0", "gqA.y1", "gqA.y2", "gqA.y3", "gqB.a0", "gqB.a1", "gqB.b0",
    "gqB.b1", "goA.f", "gkv.m0", "goB.f", "gqA.m", "gqB.m0", "gkv.p0", "u3a", "gkv.p1", "gqA.a", "u4b",
    "gqA.b", "gqB.p0", "u4a", "gqB.p1", "gqA.b_", "gkv.y", "u5", "gqA.p", "gqA.p_", "gqB.y", "gqA.f", "gkv.f",
    "ufin", "gqB.f",
)


def nn(a, b):
    return jnp.dot(a, b, preferred_element_type=F32)


def nt(a, b):
    return lax.dot_general(a, b, (((1,), (1,)), ((), ())), preferred_element_type=F32)


def tn(a, b):
    return lax.dot_general(a, b, (((0,), (0,)), ((), ())), preferred_element_type=F32)


def kernel(
    anchor, augment, lag_in, w_query, w_key, w_value, w_out, cot_in,
    update_hbm, g_query_hbm, g_key_hbm, g_value_hbm, g_out_hbm,
    anc, anc_t, sts, sts_t, cot, wq, wkv, wo,
    s_out, s_kv, s_q, upd, rz, ru,
    ra_out, rc_out, ry_out, ra_kv, rc_kv, ry_kv, ra_q, rc_q, ry_q,
    part, part_kv, other, other_kv, q_h, k_h, v_h, b_h, probs, att, ctx, qb, kvb,
    update, g_query, g_key, g_value, g_out, lag,
    send, recv, near_send, near_recv, fin_recv, local,
):
    dp, c, t = lax.axis_index("dp"), lax.axis_index("seq"), lax.axis_index("tensor")
    z, yl = t // 2, t % 2
    o = 1 - c
    xr, xl = (dp + 2) % NS, (dp + 6) % NS
    far = (dp + 4) % NS
    yp = dp + 1 - 2 * (dp % 2)
    ty = t + 1 - 2 * yl
    to_xr, to_xl, to_yp = (xr, c, t), (xl, c, t), (yp, c, t)
    to_zr, to_zl = (dp, c, (t + 2) % 16), (dp, c, (t + 14) % 16)
    to_sib = (dp, o, t)
    same = c == yl

    barrier = pltpu.get_barrier_semaphore()
    partners = (to_xr, to_xl, to_yp, to_zr, to_zl, to_sib, (dp, 0, ty), (dp, 1, ty))
    for who in partners:
        pl.semaphore_signal(barrier, inc=1, device_id=who, device_id_type=MESH)
    pl.semaphore_wait(barrier, len(partners))

    started = []
    arriving = {}
    tasks = {}

    def push(name, src, dst, who):
        i = len(started)
        copy = pltpu.make_async_remote_copy(
            src_ref=src, dst_ref=dst, send_sem=send.at[i], recv_sem=recv.at[i],
            device_id=who, device_id_type=MESH,
        )
        copy.start()
        started.append(copy)
        arriving.setdefault(name, []).append(copy)

    def wait(*names):
        for name in names:
            for copy in arriving.pop(name, ()):
                copy.wait_recv()

    locals_ = []

    def fetch(src, dst):
        copy = pltpu.make_async_copy(src, dst, local.at[len(locals_)])
        copy.start()
        locals_.append(copy)

    def col(i, n):
        return pl.ds(pl.multiple_of(i * n, n), n)

    def flip(k):
        return k + 1 - 2 * (k % 2)

    mine = pl.ds(pl.multiple_of(c * TOK, TOK), TOK)
    head = col(c, HEAD)
    head_o = col(o, HEAD)
    head_v = pl.ds(pl.multiple_of(256 + c * HEAD, HEAD), HEAD)
    head_vo = pl.ds(pl.multiple_of(256 + o * HEAD, HEAD), HEAD)

    def kv_rows(k, r0, n):
        return pl.ds(pl.multiple_of((2 * k + c) * 224 + r0, 16), n)

    def rows_of(buf):
        return lambda k, r0, n: buf.at[k, pl.ds(r0, n)]

    def slot_kv(k, r0, n):
        return wkv.at[kv_rows(k, r0, n)]

    def y_first(name, own, slot, r0, n):
        h = n // 2

        def from_y():
            wait(name + "y")
            s = slot(yp, r0, n)
            push(name + "fr", s, s, to_xr)
            push(name + "fl", s, s, to_xl)

        def near(first, second, a, b):
            def run():
                wait(name + first + "r", name + first + "l")
                lo, hi = slot(a, r0, h), slot(b, r0 + h, h)
                push(name + second + "0", lo, lo, to_xr)
                push(name + second + "1", hi, hi, to_xl)
            return run

        tasks[name + ".fy"] = from_y
        tasks[name + ".fx"] = near("", "h", xl, xr)
        tasks[name + ".fxf"] = near("f", "g", flip(xl), flip(xr))
        for src, dst in own:
            push(name + "y", src, dst, to_yp)
        for src, dst in own:
            push(name + "r", src, dst, to_xr)
            push(name + "l", src, dst, to_xl)
        return [name + e for e in ("y", "r", "l", "fr", "fl", "h0", "h1", "g0", "g1")]

    def x_first(name, own, slot, r0, n):
        h = n // 2

        def from_x():
            wait(name + "r", name + "l")
            lo, hi = slot(xl, r0, h), slot(xr, r0 + h, h)
            push(name + "h0", lo, lo, to_xr)
            push(name + "h1", hi, hi, to_xl)
            a, b = slot(xl, r0, n), slot(xr, r0, n)
            push(name + "y0", a, a, to_yp)
            push(name + "y1", b, b, to_yp)

        def from_far():
            for i in (0, 1):
                wait(name + "h%d" % i)
                s = slot(far, r0 + i * h, h)
                push(name + "g%d" % i, s, s, to_yp)

        tasks[name + ".fx"] = from_x
        tasks[name + ".fxf"] = from_far
        for src, dst in own:
            push(name + "r", src, dst, to_xr)
            push(name + "l", src, dst, to_xl)
        for src, dst in own:
            push(name + "y", src, dst, to_yp)
        return [name + e for e in ("y", "r", "l", "h0", "h1", "y0", "y1", "g0", "g1")]

    def own_rows(src, buf, r0, n):
        return [(src.at[pl.ds(r0, n)], buf.at[dp, pl.ds(r0, n)])]

    def split(name, src, buf, cut):
        n = buf.shape[1]
        names = []
        if cut:
            names += x_first(name + "A", own_rows(src, buf, 0, cut), rows_of(buf), 0, cut)
        if cut < n:
            names += y_first(name + "B", own_rows(src, buf, cut, n - cut), rows_of(buf), cut, n - cut)
        return names

    cot_dst = cot.at[z, mine]
    cot_far = pltpu.make_async_remote_copy(
        src_ref=cot_in.at[0], dst_ref=cot_dst, send_sem=near_send.at[0], recv_sem=near_recv.at[c],
        device_id=(dp, yl, ty), device_id_type=MESH)
    cot_sib = pltpu.make_async_remote_copy(
        src_ref=cot_in.at[0], dst_ref=cot_dst, send_sem=near_send.at[1], recv_sem=near_recv.at[c],
        device_id=to_sib, device_id_type=MESH)
    cot_own = pltpu.make_async_copy(cot_in.at[0], cot_dst, near_recv.at[c])
    cot_far.start()

    @pl.when(same)
    def _():
        cot_own.start()

    @pl.when(jnp.logical_not(same))
    def _():
        cot_sib.start()

    own_kv = kv_rows(dp, 0, 224)
    kv_all = y_first("kv", [(w_key, wkv.at[own_kv, pl.ds(0, 256)]), (w_value, wkv.at[own_kv, pl.ds(256, 256)])],
                     slot_kv, 0, 224)
    q_all = split("q", w_query, wq, Q_Y)
    o_all = []

    def own_o():
        o_all.extend(split("o", w_out, wo, O_Y))

    tasks["own_o"] = own_o

    push("sib", augment.at[0], sts.at[mine], to_sib)
    fetch(augment.at[0], sts.at[mine])
    for k in range(NS):
        push("sib", anchor.at[0, :, pl.ds(pl.multiple_of((2 * k + o) * 512, 512), 512)], anc.at[k, mine], to_sib)
        fetch(anchor.at[0, :, pl.ds(pl.multiple_of((2 * k + c) * 512, 512), 512)], anc.at[k, mine])
    fetch(w_query, wq.at[dp])
    fetch(w_key, wkv.at[own_kv, pl.ds(0, 256)])
    fetch(w_value, wkv.at[own_kv, pl.ds(256, 256)])
    fetch(w_out, wo.at[dp])
    fetch(lag_in, lag)

    zero = jnp.zeros((224, 512), BF)
    for k in range(NS):
        wkv[pl.ds(pl.multiple_of((2 * k + o) * 224, 224), 224), :] = zero

    lo_tok, hi_tok = pl.ds(0, TOK), pl.ds(TOK, TOK)

    def ring(step, part_):
        def run():
            a, b = (lo_tok, hi_tok) if part_ == "a" else (hi_tok, lo_tok)
            if step == 1 and part_ == "a":
                for h in (0, 1):
                    got = cot.at[z, pl.ds(h * TOK, TOK)]
                    pltpu.make_async_copy(got, got, near_recv.at[h]).wait()
            if step > 1:
                wait("Z%d%s" % (step - 1, part_))
            s, r = cot.at[(z + 9 - step) % NS, a], cot.at[(z + step - 1) % NS, b]
            push("Z%d%s" % (step, part_), s, s, to_zr)
            push("Z%d%s" % (step, part_), r, r, to_zl)
        return run

    z_all = []
    for step in range(1, 5):
        for part_ in ("a", "b") if step < 4 else ("a",):
            tasks["z%d%s" % (step, part_)] = ring(step, part_)
            z_all.append("Z%d%s" % (step, part_))

    def turn(i):
        def run():
            if i == 0:
                wait("sib")
                for copy in locals_:
                    copy.wait()
            anc_t[i] = anc[i].T
            if i < 7:
                sts_t[pl.ds(i * 512, 512), :] = sts[:, pl.ds(i * 512, 512)].T
        return run

    for i in range(NS):
        tasks["turn%d" % i] = turn(i)

    def keys_values():
        wait(*kv_all)
        part_kv[...] = nn(sts[:, pl.ds(0, 512)], wkv[pl.ds(0, 512), :])

        def add_kv(j, _):
            part_kv[...] += nn(sts[:, col(j, 512)], wkv[col(j, 512), :])
            return _

        lax.fori_loop(1, 7, add_kv, 0)
        push("exk", part_kv.at[:, head_o], other_kv.at[0], to_sib)
        push("exk", part_kv.at[:, head_vo], other_kv.at[1], to_sib)

    def queries():
        wait(*q_all)
        part[0] = nn(anc[0], wq[0])

        def add_q(k, _):
            part[0] += nn(anc[k], wq[k])
            return _

        lax.fori_loop(1, NS, add_q, 0)
        push("exq", part.at[0, :, head_o], other.at[0], to_sib)

    factor = HEAD ** (-0.5)
    block = 128

    def attend(r):
        def run():
            if r == 0:
                wait("exk")
                k_h[...] = (part_kv[:, head] + other_kv[0]).astype(BF)
                v_h[...] = (part_kv[:, head_v] + other_kv[1]).astype(BF)
                wait("exq")
                q_h[...] = (part[0, :, head] + other[0]).astype(BF)
            rows = pl.ds(r * block, block)
            scores = nt(q_h[rows, :], k_h[...]) * factor
            reach = lax.broadcasted_iota(jnp.int32, (block, LEN), 0) + (r * block + lag[0])
            allowed = lax.broadcasted_iota(jnp.int32, (block, LEN), 1) <= reach
            scores = jnp.where(allowed, scores, -jnp.inf)
            expo = jnp.exp(scores - jnp.max(scores, axis=1, keepdims=True))
            p = expo / jnp.sum(expo, axis=1, keepdims=True)
            probs[rows, :] = p
            a = p.astype(BF)
            att[rows, :] = a
            ctx[rows, head] = nn(a, v_h[...]).astype(BF)
            if r == LEN // block - 1:
                push("ectx", ctx.at[:, head], ctx.at[:, head], to_sib)
        return run

    tasks["kv"] = keys_values
    tasks["q"] = queries
    for r in range(LEN // block):
        tasks["attn%d" % r] = attend(r)

    def back_context():
        wait(*o_all)
        wait(*z_all)
        part[1] = nt(cot[0], wo[0])

        def add_b(k, _):
            part[1] += nt(cot[k], wo[k])
            return _

        lax.fori_loop(1, NS, add_b, 0)
        push("eb", part.at[1, :, head_o], other.at[1], to_sib)

    tasks["bc"] = back_context

    def backward(r):
        def run():
            if r == 0:
                wait("eb")
                b_h[...] = (part[1, :, head] + other[1]).astype(BF)
            rows = pl.ds(r * block, block)
            dprobs = nt(b_h[rows, :], v_h[...])
            delta = jnp.sum(b_h[rows, :].astype(F32) * ctx[rows, head].astype(F32), axis=1, keepdims=True)
            ds = (probs[rows, :] * (dprobs - delta) * factor).astype(BF)
            qb[rows, head] = nn(ds, k_h[...]).astype(BF)
            kt = tn(ds, q_h[rows, :])
            vt = tn(att[rows, :], b_h[rows, :])
            if r == 0:
                other_kv[0] = kt
                other_kv[1] = vt
            else:
                other_kv[0] += kt
                other_kv[1] += vt
            if r == LEN // block - 1:
                kvb[:, head] = other_kv[0].astype(BF)
                kvb[:, head_v] = other_kv[1].astype(BF)
                push("ekb", kvb.at[:, head], kvb.at[:, head], to_sib)
                push("ekb", kvb.at[:, head_v], kvb.at[:, head_v], to_sib)
                push("ekb", qb.at[:, head], qb.at[:, head], to_sib)
        return run

    for r in range(LEN // block):
        tasks["bwd%d" % r] = backward(r)

    def slot(off, j):
        k = (dp + 2 * off + NS) % NS
        return flip(k) if j else k

    def add(s, k, rows, got):
        s[k, rows] = (s[k, rows].astype(F32) + got.astype(F32)).astype(BF)

    def sum_x_first(name, ready, s, r0, n, ra, rc, ry, make, out):
        h = n // 2
        lo, hi = pl.ds(r0, h), pl.ds(r0 + h, h)
        full = pl.ds(r0, n)

        def first(j):
            def run():
                ready()
                k = slot(2, j)
                make(k, r0, n)
                push(name + "a%d" % j, s.at[k, lo], ra.at[0, j], to_xr)
                push(name + "a%d" % j, s.at[k, hi], ra.at[1, j], to_xl)
            return run

        def second(j):
            def run():
                k, m = slot(1, j), slot(-1, j)
                make(k, r0, n)
                push(name + "b%d" % j, s.at[k, hi], rc.at[0, j, pl.ds(h, h)], to_xr)
                make(m, r0, n)
                push(name + "b%d" % j, s.at[m, lo], rc.at[1, j, pl.ds(0, h)], to_xl)
            return run

        def own():
            make(slot(0, 1), r0, n)
            make(slot(0, 0), r0, n)

        def on(j):
            def run():
                wait(name + "a%d" % j)
                k, m = slot(1, j), slot(-1, j)
                add(s, k, lo, ra[0, j])
                push(name + "p%d" % j, s.at[k, lo], rc.at[0, j, pl.ds(0, h)], to_xr)
                add(s, m, hi, ra[1, j])
                push(name + "p%d" % j, s.at[m, hi], rc.at[1, j, pl.ds(h, h)], to_xl)
            return run

        def total(j):
            wait(name + "b%d" % j, name + "p%d" % j)
            return s[slot(0, j), full].astype(F32) + rc[0, j].astype(F32) + rc[1, j].astype(F32)

        def across():
            k = slot(0, 1)
            s[k, full] = total(1).astype(BF)
            push(name + "y", s.at[k, full], ry, to_yp)

        def finish():
            both = total(0)
            wait(name + "y")
            out(both + ry[...].astype(F32), r0, n)

        for j in (0, 1):
            tasks[name + ".a%d" % j] = first(j)
            tasks[name + ".b%d" % j] = second(j)
            tasks[name + ".p%d" % j] = on(j)
        tasks[name + ".m0"] = own
        tasks[name + ".y"] = across
        tasks[name + ".f"] = finish

    def sum_y_first(name, ready, s, r0, n, ra, rc, ry, make, out):
        h = n // 2
        lo, hi = pl.ds(r0, h), pl.ds(r0 + h, h)
        full = pl.ds(r0, n)
        offs = (2, 1, -1, 0)

        def first(i):
            def run():
                ready()
                k = slot(offs[i], 1)
                make(k, r0, n)
                push(name + "y%d" % i, s.at[k, full], ry.at[i], to_yp)
            return run

        def own():
            for off in offs:
                make(slot(off, 0), r0, n)

        def from_y():
            wait(name + "y0")
            k = slot(2, 0)
            add(s, k, full, ry[0])
            push(name + "a", s.at[k, lo], ra.at[0], to_xr)
            push(name + "a_", s.at[k, hi], ra.at[1], to_xl)

        def right():
            wait(name + "y1")
            k = slot(1, 0)
            add(s, k, full, ry[1])
            push(name + "b", s.at[k, hi], rc.at[0, pl.ds(h, h)], to_xr)

        def left():
            wait(name + "y2")
            m = slot(-1, 0)
            add(s, m, full, ry[2])
            push(name + "b", s.at[m, lo], rc.at[1, pl.ds(0, h)], to_xl)

        def on_right():
            wait(name + "a")
            k = slot(1, 0)
            add(s, k, lo, ra[0])
            push(name + "p", s.at[k, lo], rc.at[0, pl.ds(0, h)], to_xr)

        def on_left():
            wait(name + "a_")
            m = slot(-1, 0)
            add(s, m, hi, ra[1])
            push(name + "p", s.at[m, hi], rc.at[1, pl.ds(h, h)], to_xl)

        def finish():
            wait(name + "y3", name + "b", name + "p")
            k = slot(0, 0)
            out(s[k, full].astype(F32) + ry[3].astype(F32) + rc[0].astype(F32) + rc[1].astype(F32), r0, n)

        for i in range(4):
            tasks[name + ".y%d" % i] = first(i)
        tasks[name + ".m"] = own
        tasks[name + ".a"] = from_y
        tasks[name + ".b"] = right
        tasks[name + ".b_"] = left
        tasks[name + ".p"] = on_right
        tasks[name + ".p_"] = on_left
        tasks[name + ".f"] = finish

    written = []

    def write(src, dst):
        copy = pltpu.make_async_copy(src, dst, fin_recv.at[2 + len(written)])
        copy.start()
        written.append(copy)

    def make_out(k, r0, n):
        s_out[k, pl.ds(r0, n)] = tn(ctx[:, pl.ds(r0, n)], cot[k]).astype(BF)

    def put_out(total, r0, n):
        g_out[pl.ds(r0, n)] = total.astype(BF)
        write(g_out.at[pl.ds(r0, n)], g_out_hbm.at[pl.ds(r0, n)])

    def make_kv(k, r0, n):
        s_kv[k] = nn(sts_t[pl.ds(pl.multiple_of((2 * k + c) * 224, 224), 224), :], kvb[...]).astype(BF)

    def put_kv(total, r0, n):
        g_key[...] = total[:, :256].astype(BF)
        g_value[...] = total[:, 256:].astype(BF)
        write(g_key, g_key_hbm)
        write(g_value, g_value_hbm)

    def make_q(k, r0, n):
        s_q[k, pl.ds(r0, n)] = nn(anc_t[k, pl.ds(r0, n), :], qb[...]).astype(BF)

    def put_q(total, r0, n):
        g_query[pl.ds(r0, n)] = total.astype(BF)
        write(g_query.at[pl.ds(r0, n)], g_query_hbm.at[pl.ds(r0, n)])

    def ctx_ready():
        wait(*z_all)
        wait("ectx")

    def back_ready():
        wait("ekb")

    ra_oa, ra_ob = ra_out
    rc_oa, rc_ob = rc_out
    ry_oa, ry_ob = ry_out
    ra_qa, ra_qb = ra_q
    rc_qa, rc_qb = rc_q
    ry_qa, ry_qb = ry_q
    if GO_Y:
        sum_y_first("goA", ctx_ready, s_out, 0, GO_Y, ra_oa, rc_oa, ry_oa, make_out, put_out)
    if GO_Y < 256:
        sum_x_first("goB", ctx_ready, s_out, GO_Y, 256 - GO_Y, ra_ob, rc_ob, ry_ob, make_out, put_out)
    sum_x_first("gkv", back_ready, s_kv, 0, 224, ra_kv, rc_kv, ry_kv, make_kv, put_kv)
    if GQ_Y:
        sum_y_first("gqA", back_ready, s_q, 0, GQ_Y, ra_qa, rc_qa, ry_qa, make_q, put_q)
    if GQ_Y < 512:
        sum_x_first("gqB", back_ready, s_q, GQ_Y, 512 - GQ_Y, ra_qb, rc_qb, ry_qb, make_q, put_q)

    def ring_add(step, part_):
        def run():
            a, b = (lo_tok, hi_tok) if part_ == "a" else (hi_tok, lo_tok)
            k, m = (z + 5 - step) % NS, (z + 3 + step) % NS
            if step > 1 and (step, part_) != (2, "b"):
                wait("U%d%s" % (step - 1, part_))
                add(upd, k, a, rz[0, step - 2, a])
                push("U%d%s" % (step, part_), upd.at[k, a], rz.at[0, step - 1, a], to_zr)
                add(upd, m, b, rz[1, step - 2, b])
                push("U%d%s" % (step, part_), upd.at[m, b], rz.at[1, step - 1, b], to_zl)
            else:
                push("U%d%s" % (step, part_), upd.at[k, a], rz.at[0, step - 1, a], to_zr)
                push("U%d%s" % (step, part_), upd.at[m, b], rz.at[1, step - 1, b], to_zl)
        return run

    def updates():
        wait("ectx")
        wait(*o_all)

        def make_upd(k, _):
            upd[k] = nn(ctx[...], wo[k]).astype(BF)
            return _

        lax.fori_loop(0, NS, make_upd, 0)
        ring_add(1, "a")()
        ring_add(2, "b")()

    tasks["upd"] = updates
    for step in (2, 3, 4):
        for part_ in ("a", "b"):
            if (step, part_) != (2, "b"):
                tasks["u%d%s" % (step, part_)] = ring_add(step, part_)

    given = upd.at[z, pl.ds(pl.multiple_of(o * TOK, TOK), TOK)]
    fin_own = pltpu.make_async_copy(upd.at[z, mine], ru.at[0], fin_recv.at[0])
    fin_sib = pltpu.make_async_remote_copy(
        src_ref=given, dst_ref=ru.at[0], send_sem=near_send.at[2], recv_sem=fin_recv.at[0],
        device_id=to_sib, device_id_type=MESH)
    fin_far = [
        pltpu.make_async_remote_copy(
            src_ref=upd.at[z, pl.ds(h * TOK, TOK)], dst_ref=ru.at[1], send_sem=near_send.at[3 + h],
            recv_sem=fin_recv.at[1], device_id=(dp, h, ty), device_id_type=MESH)
        for h in (0, 1)
    ]

    def last_exchange():
        wait("U4a", "U4b")
        upd[z] = (upd[z].astype(F32) + rz[0, 3].astype(F32) + rz[1, 3].astype(F32)).astype(BF)

        @pl.when(same)
        def _():
            fin_own.start()
            fin_sib.start()

        @pl.when(jnp.logical_not(same))
        def _():
            fin_far[0].start()
            fin_far[1].start()

    def last_sum():
        for i in (0, 1):
            pltpu.make_async_copy(ru.at[i], ru.at[i], fin_recv.at[i]).wait()
        update[0] = (ru[0].astype(F32) + ru[1].astype(F32)).astype(BF)
        write(update, update_hbm)

    tasks["u5"] = last_exchange
    tasks["ufin"] = last_sum

    for name in ORDER:
        tasks.pop(name)()
    assert not tasks and not arriving

    for copy in started:
        copy.wait_send()
    cot_far.wait_send()

    @pl.when(jnp.logical_not(same))
    def _():
        cot_sib.wait_send()
        fin_far[0].wait_send()
        fin_far[1].wait_send()

    @pl.when(same)
    def _():
        fin_sib.wait_send()

    for copy in written:
        copy.wait()


def hand_on(*refs):
    for i in range(5):
        refs[5 + i][...] = refs[i][...]


def local(*args):
    vm = pltpu.VMEM
    shapes = [
        ((1, TOK, 512), BF), ((512, 256), BF), ((224, 256), BF), ((224, 256), BF), ((256, 512), BF),
    ]

    def landing(n, width, cut):
        a, b = max(cut, 32), max(n - cut, 32)
        ra = [vm((2, a // 2, width), BF), vm((2, 2, b // 2, width), BF)]
        rc = [vm((2, a, width), BF), vm((2, 2, b, width), BF)]
        ry = [vm((4, a, width), BF), vm((b, width), BF)]
        return [ra, rc, ry]

    scratch = [
        vm((NS, LEN, 512), BF), vm((NS, 512, LEN), BF), vm((LEN, 3584), BF), vm((3584, LEN), BF),
        vm((NS, LEN, 512), BF), vm((NS, 512, 256), BF), vm((3584, 512), BF), vm((NS, 256, 512), BF),
        vm((NS, 256, 512), BF), vm((NS, 224, 512), BF), vm((NS, 512, 256), BF),
        vm((NS, LEN, 512), BF), vm((2, 4, LEN, 512), BF), vm((2, TOK, 512), BF),
        *landing(256, 512, GO_Y),
        vm((2, 2, 112, 512), BF), vm((2, 2, 224, 512), BF), vm((224, 512), BF),
        *landing(512, 256, GQ_Y),
        vm((2, LEN, 256), F32), vm((LEN, 512), F32), vm((2, LEN, HEAD), F32), vm((2, LEN, HEAD), F32),
        vm((LEN, HEAD), BF), vm((LEN, HEAD), BF), vm((LEN, HEAD), BF), vm((LEN, HEAD), BF),
        vm((LEN, LEN), F32), vm((LEN, LEN), BF), vm((LEN, 256), BF), vm((LEN, 256), BF), vm((LEN, 512), BF),
        vm((1, TOK, 512), BF), vm((512, 256), BF), vm((224, 256), BF), vm((224, 256), BF), vm((256, 512), BF),
        pltpu.SMEM((1,), jnp.int32),
        pltpu.SemaphoreType.DMA((COPIES,)), pltpu.SemaphoreType.DMA((COPIES,)),
        pltpu.SemaphoreType.DMA((5,)), pltpu.SemaphoreType.DMA((2,)), pltpu.SemaphoreType.DMA((9,)),
        pltpu.SemaphoreType.DMA((16,)),
    ]
    any_ = pl.BlockSpec(memory_space=pl.ANY)
    vmem = pl.BlockSpec(memory_space=pltpu.VMEM)
    results = [jax.ShapeDtypeStruct(s, d) for s, d in shapes]
    outs = pl.pallas_call(
        kernel,
        out_shape=results,
        in_specs=[any_] * 8,
        out_specs=[any_] * 5,
        scratch_shapes=scratch,
        compiler_params=pltpu.CompilerParams(
            collective_id=0, has_side_effects=True, vmem_limit_bytes=58 * 2**20
        ),
        name="block",
    )(*args)
    return pl.pallas_call(
        hand_on,
        out_shape=results,
        in_specs=[vmem] * 5,
        out_specs=[vmem] * 5,
        name="hand_on",
    )(*outs)


def solution(mesh):
    placed = (
        P("dp", "seq", None),
        P("dp", "seq", None),
        P("dp"),
        P(("dp", "seq"), "tensor"),
        P(("dp", "seq"), "tensor"),
        P(("dp", "seq"), "tensor"),
        P("tensor", ("dp", "seq")),
        P("dp", "seq", "tensor"),
    )
    return jax.shard_map(
        local,
        mesh=mesh,
        in_specs=placed,
        out_specs=(
            P("dp", "seq", "tensor"),
            P(("dp", "seq"), "tensor"),
            P(("dp", "seq"), "tensor"),
            P(("dp", "seq"), "tensor"),
            P("tensor", ("dp", "seq")),
        ),
        check_vma=False,
    )
```

time: 748 us -> 108 us (0.14)
  waiting for transfers between devices: 676 us -> 0 us
  Pallas kernels: 0 us -> 107 us
  matrix products: 38.5 us -> 0 us
  local copies, waits for them, and re-layouts: 15.7 us -> 0 us
  between operations: 15 us -> 1.29 us
    all_gather x6 -> x0, waiting for transfers between devices: 323 us -> none  [the longest x1 72.3 us: local(): cotangent_full = lax.all_gather(cotangent, 'tensor', axis=2, tiled=True)[0]]
    reduce_scatter x3 -> x0, waiting for transfers between devices: 244 us -> none  [the longest x1 94.8 us: local(): lax.psum_scatter(contract_first(context, cotangent_full).astype(jnp.bfloa...]
    unnamed x15 -> x0, waiting for transfers between devices: 109 us -> none
    pallas_call x0 -> x2, Pallas kernels: none -> 107 us  [the longest x1 105 us: local(): pl.pallas_call(kernel, out_shape=results, in_specs=[any_] * 8, out_specs=...]
    dot_general x13 -> x0, matrix products: 37.3 us -> none  [the longest x3 12.9 us: contract_first(): lax.dot_general(left, right, (((0,), (0,)), ((), ())), preferred_element_...]
    unnamed x18 -> x0, local copies, waits for them, and re-layouts: 14.1 us -> none
  transfers between devices with their start and end apart: 12 -> 0, of which waited for: 12 -> 0; matrix products, arithmetic and copies ran while one was open for 7% -> 0% of each run, Pallas kernels for 0% -> 0%
where the time goes in v2:
time: 108 us
  Pallas kernels  107 us (99%)
  between operations  1.29 us (1%)
    pallas_call x1, Pallas kernels, local(): pl.pallas_call(kernel, out_shape=results, in_specs=[any_] * 8, out_specs=...  105 us
    pallas_call x1, Pallas kernels, local(): pl.pallas_call(hand_on, out_shape=results, in_specs=[vmem] * 5, out_specs...  2.16 us

profile of v2, /device:TPU:1, one launch (start us, length us, event | category | flops | bytes accessed | tf_op | source)
XLA Modules:
  0.0 108.1 jit_solution(15751689909113205557)
XLA Ops:
  1.3 104.7 %block.1 = (bf16[1,192,512]{2,1,0:T(8,128)(2,1)}, bf16[512,256]{1,0:T(8,128)(2,1)}, bf16[224,256]{1,0:T(8,128)(2,1)}, bf16[224,256]{1,0:T(8,128)(2,1)}, bf16[256,512]{1,0:T(8,128)(2,1)}) custom-call(bf16[1,192,8192]{2,1,0:T(8,128)(2,1)} %anchor.1, bf16[1,192,3584]{2,1,0:T(8,128)(2,1)} %augment.1, s32[1]{0:T(128)S(6)} %copy.13.lag_in, ...), custom_call_target="tpu_custom_call" | custom-call | tf_op jit(solution)/shard_map/block/pallas_call | solution.py:673
  106.0 2.2 %hand_on.1 = (bf16[1,192,512]{2,1,0:T(8,128)(2,1)}, bf16[512,256]{1,0:T(8,128)(2,1)}, bf16[224,256]{1,0:T(8,128)(2,1)}, bf16[224,256]{1,0:T(8,128)(2,1)}, bf16[256,512]{1,0:T(8,128)(2,1)}) custom-call(bf16[1,192,512]{2,1,0:T(8,128)(2,1)} %get-tuple-element.10.refs_0_, bf16[512,256]{1,0:T(8,128)(2,1)} %get-tuple-element.11.refs_1_, ...), custom_call_target="tpu_custom_call" | custom-call | tf_op jit(solution)/shard_map/hand_on/pallas_call | solution.py:684

commit v3 on v2

--- a/solution.py
+++ b/solution.py
@@ -14,18 +14,21 @@
 NS = 8
 COPIES = 256
 
-Q_Y, O_Y, GQ_Y, GO_Y = 384, 128, 320, 128
+Q_Y, O_Y, GQ_Y, GO_Y = 416, 96, 416, 128
+
+FIRST = ('kv', 'qA', 'qB')
+O_LAST_Y = 1
 
 ORDER = (
     "z1a", "z1b", "kv.fx", "kv.fy", "qA.fx", "qB.fx", "z2a", "turn0", "turn1", "turn2", "turn3", "turn4",
-    "qB.fy", "turn5", "z2b", "turn6", "turn7", "kv.fxf", "z3a", "qA.fxf", "own_o", "qB.fxf", "z3b", "kv",
-    "oA.fx", "z4a", "oB.fx", "q", "oA.fxf", "oB.fy", "attn0", "attn1", "attn2", "oB.fxf", "goA.y0", "goA.y1",
-    "goA.y2", "goA.y3", "goB.a0", "goB.a1", "goB.b0", "goB.b1", "goA.m", "goB.m0", "bc", "upd", "goB.p0",
-    "goA.a", "goB.p1", "bwd0", "bwd1", "goA.b", "bwd2", "u2a", "goA.b_", "goA.p", "goA.p_", "goB.y", "gkv.a0",
-    "gkv.a1", "gkv.b0", "gkv.b1", "u3b", "gqA.y0", "gqA.y1", "gqA.y2", "gqA.y3", "gqB.a0", "gqB.a1", "gqB.b0",
-    "gqB.b1", "goA.f", "gkv.m0", "goB.f", "gqA.m", "gqB.m0", "gkv.p0", "u3a", "gkv.p1", "gqA.a", "u4b",
-    "gqA.b", "gqB.p0", "u4a", "gqB.p1", "gqA.b_", "gkv.y", "u5", "gqA.p", "gqA.p_", "gqB.y", "gqA.f", "gkv.f",
-    "ufin", "gqB.f",
+    "turn5", "qB.fy", "turn6", "z2b", "turn7", "kv.fxf", "z3a", "qA.fxf", "own_o", "qB.fxf", "z3b", "kv",
+    "z4a", "oB.fx", "oA.fx", "q", "oB.fy", "oA.fxf", "attn0", "attn1", "attn2", "oB.fxf", "goA.y0", "goA.y1",
+    "goA.y2", "goA.y3", "goB.a0", "goB.a1", "goB.b0", "goB.b1", "goA.m", "goB.m0", "bc", "upd", "goA.a",
+    "goB.p0", "goB.p1", "bwd0", "bwd1", "bwd2", "goA.b", "goA.b_", "goA.p", "goA.p_", "u2a", "goB.y",
+    "gkv.a0", "gkv.a1", "gqA.y0", "gqA.y1", "gqA.y2", "gqA.y3", "gkv.b0", "gkv.b1", "u3b", "gqB.a0", "gqB.a1",
+    "gqB.b0", "gqB.b1", "gkv.m0", "gqA.m", "goA.f", "goB.f", "gqB.m0", "gkv.p0", "u3a", "gkv.p1", "gqA.a",
+    "u4b", "gqB.p0", "gqA.b", "gqB.p1", "u4a", "gqA.b_", "gkv.y", "gqA.p", "gqA.p_", "u5", "gqB.y", "gkv.f",
+    "gqA.f", "ufin", "gqB.f",
 )
 
 
@@ -43,12 +46,12 @@
 
 def kernel(
     anchor, augment, lag_in, w_query, w_key, w_value, w_out, cot_in,
-    update_hbm, g_query_hbm, g_key_hbm, g_value_hbm, g_out_hbm,
+    update, g_query, g_key, g_value, g_out,
     anc, anc_t, sts, sts_t, cot, wq, wkv, wo,
     s_out, s_kv, s_q, upd, rz, ru,
     ra_out, rc_out, ry_out, ra_kv, rc_kv, ry_kv, ra_q, rc_q, ry_q,
     part, part_kv, other, other_kv, q_h, k_h, v_h, b_h, probs, att, ctx, qb, kvb,
-    update, g_query, g_key, g_value, g_out, lag,
+    lag, stage,
     send, recv, near_send, near_recv, fin_recv, local,
 ):
     dp, c, t = lax.axis_index("dp"), lax.axis_index("seq"), lax.axis_index("tensor")
@@ -67,7 +70,6 @@
     partners = (to_xr, to_xl, to_yp, to_zr, to_zl, to_sib, (dp, 0, ty), (dp, 1, ty))
     for who in partners:
         pl.semaphore_signal(barrier, inc=1, device_id=who, device_id_type=MESH)
-    pl.semaphore_wait(barrier, len(partners))
 
     started = []
     arriving = {}
@@ -116,8 +118,9 @@
     def slot_kv(k, r0, n):
         return wkv.at[kv_rows(k, r0, n)]
 
-    def y_first(name, own, slot, r0, n):
+    def y_first(name, slot, r0, n):
         h = n // 2
+        mine_ = slot(dp, r0, n)
 
         def from_y():
             wait(name + "y")
@@ -136,15 +139,14 @@
         tasks[name + ".fy"] = from_y
         tasks[name + ".fx"] = near("", "h", xl, xr)
         tasks[name + ".fxf"] = near("f", "g", flip(xl), flip(xr))
-        for src, dst in own:
-            push(name + "y", src, dst, to_yp)
-        for src, dst in own:
-            push(name + "r", src, dst, to_xr)
-            push(name + "l", src, dst, to_xl)
+        push(name + "y", mine_, mine_, to_yp)
+        push(name + "r", mine_, mine_, to_xr)
+        push(name + "l", mine_, mine_, to_xl)
         return [name + e for e in ("y", "r", "l", "fr", "fl", "h0", "h1", "g0", "g1")]
 
-    def x_first(name, own, slot, r0, n):
+    def x_first(name, slot, r0, n):
         h = n // 2
+        mine_ = slot(dp, r0, n)
 
         def from_x():
             wait(name + "r", name + "l")
@@ -163,33 +165,31 @@
 
         tasks[name + ".fx"] = from_x
         tasks[name + ".fxf"] = from_far
-        for src, dst in own:
-            push(name + "r", src, dst, to_xr)
-            push(name + "l", src, dst, to_xl)
-        for src, dst in own:
-            push(name + "y", src, dst, to_yp)
+        push(name + "r", mine_, mine_, to_xr)
+        push(name + "l", mine_, mine_, to_xl)
+        push(name + "y", mine_, mine_, to_yp)
         return [name + e for e in ("y", "r", "l", "h0", "h1", "y0", "y1", "g0", "g1")]
 
-    def own_rows(src, buf, r0, n):
-        return [(src.at[pl.ds(r0, n)], buf.at[dp, pl.ds(r0, n)])]
-
-    def split(name, src, buf, cut):
-        n = buf.shape[1]
-        names = []
-        if cut:
-            names += x_first(name + "A", own_rows(src, buf, 0, cut), rows_of(buf), 0, cut)
-        if cut < n:
-            names += y_first(name + "B", own_rows(src, buf, cut, n - cut), rows_of(buf), cut, n - cut)
-        return names
+    own_kv = kv_rows(dp, 0, 224)
+    fetch(cot_in.at[0], stage)
+    fetch(w_key, wkv.at[own_kv, pl.ds(0, 256)])
+    fetch(w_value, wkv.at[own_kv, pl.ds(256, 256)])
+    fetch(w_query, wq.at[dp])
+    fetch(w_out, wo.at[dp])
+    early = len(locals_)
+    fetch(lag_in, lag)
+    for copy in locals_[:early]:
+        copy.wait()
+    pl.semaphore_wait(barrier, len(partners))
 
     cot_dst = cot.at[z, mine]
     cot_far = pltpu.make_async_remote_copy(
-        src_ref=cot_in.at[0], dst_ref=cot_dst, send_sem=near_send.at[0], recv_sem=near_recv.at[c],
+        src_ref=stage, dst_ref=cot_dst, send_sem=near_send.at[0], recv_sem=near_recv.at[c],
         device_id=(dp, yl, ty), device_id_type=MESH)
     cot_sib = pltpu.make_async_remote_copy(
-        src_ref=cot_in.at[0], dst_ref=cot_dst, send_sem=near_send.at[1], recv_sem=near_recv.at[c],
+        src_ref=stage, dst_ref=cot_dst, send_sem=near_send.at[1], recv_sem=near_recv.at[c],
         device_id=to_sib, device_id_type=MESH)
-    cot_own = pltpu.make_async_copy(cot_in.at[0], cot_dst, near_recv.at[c])
+    cot_own = pltpu.make_async_copy(stage, cot_dst, near_recv.at[c])
     cot_far.start()
 
     @pl.when(same)
@@ -200,14 +200,34 @@
     def _():
         cot_sib.start()
 
-    own_kv = kv_rows(dp, 0, 224)
-    kv_all = y_first("kv", [(w_key, wkv.at[own_kv, pl.ds(0, 256)]), (w_value, wkv.at[own_kv, pl.ds(256, 256)])],
-                     slot_kv, 0, 224)
-    q_all = split("q", w_query, wq, Q_Y)
-    o_all = []
+    kv_all, q_all, o_all = [], [], []
+
+    def gather_q_a():
+        if Q_Y:
+            q_all.extend(x_first("qA", rows_of(wq), 0, Q_Y))
+
+    def gather_q_b():
+        if Q_Y < 512:
+            q_all.extend(y_first("qB", rows_of(wq), Q_Y, 512 - Q_Y))
+
+    def gather_kv():
+        kv_all.extend(y_first("kv", slot_kv, 0, 224))
+
+    first = {"kv": gather_kv, "qA": gather_q_a, "qB": gather_q_b}
+    for name in FIRST:
+        first[name]()
+
+    def gather_o_a():
+        if O_Y:
+            o_all.extend(x_first("oA", rows_of(wo), 0, O_Y))
+
+    def gather_o_b():
+        if O_Y < 256:
+            o_all.extend(y_first("oB", rows_of(wo), O_Y, 256 - O_Y))
 
     def own_o():
-        o_all.extend(split("o", w_out, wo, O_Y))
+        for run in (gather_o_b, gather_o_a) if O_LAST_Y else (gather_o_a, gather_o_b):
+            run()
 
     tasks["own_o"] = own_o
 
@@ -216,11 +236,6 @@
     for k in range(NS):
         push("sib", anchor.at[0, :, pl.ds(pl.multiple_of((2 * k + o) * 512, 512), 512)], anc.at[k, mine], to_sib)
         fetch(anchor.at[0, :, pl.ds(pl.multiple_of((2 * k + c) * 512, 512), 512)], anc.at[k, mine])
-    fetch(w_query, wq.at[dp])
-    fetch(w_key, wkv.at[own_kv, pl.ds(0, 256)])
-    fetch(w_value, wkv.at[own_kv, pl.ds(256, 256)])
-    fetch(w_out, wo.at[dp])
-    fetch(lag_in, lag)
 
     zero = jnp.zeros((224, 512), BF)
     for k in range(NS):
@@ -252,7 +267,7 @@
         def run():
             if i == 0:
                 wait("sib")
-                for copy in locals_:
+                for copy in locals_[early:]:
                     copy.wait()
             anc_t[i] = anc[i].T
             if i < 7:
@@ -489,19 +504,11 @@
         tasks[name + ".p_"] = on_left
         tasks[name + ".f"] = finish
 
-    written = []
-
-    def write(src, dst):
-        copy = pltpu.make_async_copy(src, dst, fin_recv.at[2 + len(written)])
-        copy.start()
-        written.append(copy)
-
     def make_out(k, r0, n):
         s_out[k, pl.ds(r0, n)] = tn(ctx[:, pl.ds(r0, n)], cot[k]).astype(BF)
 
     def put_out(total, r0, n):
         g_out[pl.ds(r0, n)] = total.astype(BF)
-        write(g_out.at[pl.ds(r0, n)], g_out_hbm.at[pl.ds(r0, n)])
 
     def make_kv(k, r0, n):
         s_kv[k] = nn(sts_t[pl.ds(pl.multiple_of((2 * k + c) * 224, 224), 224), :], kvb[...]).astype(BF)
@@ -509,15 +516,12 @@
     def put_kv(total, r0, n):
         g_key[...] = total[:, :256].astype(BF)
         g_value[...] = total[:, 256:].astype(BF)
-        write(g_key, g_key_hbm)
-        write(g_value, g_value_hbm)
 
     def make_q(k, r0, n):
         s_q[k, pl.ds(r0, n)] = nn(anc_t[k, pl.ds(r0, n), :], qb[...]).astype(BF)
 
     def put_q(total, r0, n):
         g_query[pl.ds(r0, n)] = total.astype(BF)
-        write(g_query.at[pl.ds(r0, n)], g_query_hbm.at[pl.ds(r0, n)])
 
     def ctx_ready():
         wait(*z_all)
@@ -605,7 +609,6 @@
         for i in (0, 1):
             pltpu.make_async_copy(ru.at[i], ru.at[i], fin_recv.at[i]).wait()
         update[0] = (ru[0].astype(F32) + ru[1].astype(F32)).astype(BF)
-        write(update, update_hbm)
 
     tasks["u5"] = last_exchange
     tasks["ufin"] = last_sum
@@ -628,13 +631,13 @@
     def _():
         fin_sib.wait_send()
 
-    for copy in written:
+
+def hand_on(*refs):
+    copies = [pltpu.make_async_copy(refs[i], refs[5 + i], refs[10].at[i]) for i in range(5)]
+    for copy in copies:
+        copy.start()
+    for copy in copies:
         copy.wait()
-
-
-def hand_on(*refs):
-    for i in range(5):
-        refs[5 + i][...] = refs[i][...]
 
 
 def local(*args):
@@ -661,10 +664,9 @@
         vm((2, LEN, 256), F32), vm((LEN, 512), F32), vm((2, LEN, HEAD), F32), vm((2, LEN, HEAD), F32),
         vm((LEN, HEAD), BF), vm((LEN, HEAD), BF), vm((LEN, HEAD), BF), vm((LEN, HEAD), BF),
         vm((LEN, LEN), F32), vm((LEN, LEN), BF), vm((LEN, 256), BF), vm((LEN, 256), BF), vm((LEN, 512), BF),
-        vm((1, TOK, 512), BF), vm((512, 256), BF), vm((224, 256), BF), vm((224, 256), BF), vm((256, 512), BF),
-        pltpu.SMEM((1,), jnp.int32),
+        pltpu.SMEM((1,), jnp.int32), vm((TOK, 512), BF),
         pltpu.SemaphoreType.DMA((COPIES,)), pltpu.SemaphoreType.DMA((COPIES,)),
-        pltpu.SemaphoreType.DMA((5,)), pltpu.SemaphoreType.DMA((2,)), pltpu.SemaphoreType.DMA((9,)),
+        pltpu.SemaphoreType.DMA((5,)), pltpu.SemaphoreType.DMA((2,)), pltpu.SemaphoreType.DMA((2,)),
         pltpu.SemaphoreType.DMA((16,)),
     ]
     any_ = pl.BlockSpec(memory_space=pl.ANY)
@@ -672,20 +674,22 @@
     results = [jax.ShapeDtypeStruct(s, d) for s, d in shapes]
     outs = pl.pallas_call(
         kernel,
-        out_shape=results,
-        in_specs=[any_] * 8,
-        out_specs=[any_] * 5,
+        out_shape=[pltpu.VMEM(s, d) for s, d in shapes],
+        in_specs=[any_, any_, pl.BlockSpec(memory_space=pltpu.HBM)] + [any_] * 5,
+        out_specs=[vmem] * 5,
         scratch_shapes=scratch,
         compiler_params=pltpu.CompilerParams(
-            collective_id=0, has_side_effects=True, vmem_limit_bytes=58 * 2**20
+            collective_id=0, has_side_effects=True, vmem_limit_bytes=56 * 2**20
         ),
         name="block",
     )(*args)
+    outs = [pltpu.with_memory_space_constraint(out, pltpu.VMEM) for out in outs]
     return pl.pallas_call(
         hand_on,
         out_shape=results,
         in_specs=[vmem] * 5,
-        out_specs=[vmem] * 5,
+        out_specs=[any_] * 5,
+        scratch_shapes=[pltpu.SemaphoreType.DMA((5,))],
         name="hand_on",
     )(*outs)
 

time: 108 us -> 103 us (0.954)
  Pallas kernels: 107 us -> 102 us
    pallas_call x1, Pallas kernels: 105 us -> 101 us  [local(): pl.pallas_call(kernel, out_shape=[pltpu.VMEM(s, d) for s, d in shapes], i...]
    pallas_call x1, Pallas kernels: 2.16 us -> 0.98 us  [local(): pl.pallas_call(hand_on, out_shape=results, in_specs=[vmem] * 5, out_specs...]
where the time goes in v3:
time: 103 us
  Pallas kernels  102 us (99%)
  between operations  1.29 us (1%)
    pallas_call x1, Pallas kernels, local(): pl.pallas_call(kernel, out_shape=[pltpu.VMEM(s, d) for s, d in shapes], i...  101 us

profile of v3, /device:TPU:1, one launch (start us, length us, event | category | flops | bytes accessed | tf_op | source)
XLA Modules:
  0.0 103.3 jit_solution(3532527646150418898)
XLA Ops:
  1.3 101.1 %block.1 = (bf16[1,192,512]{2,1,0:T(8,128)(2,1)S(1)}, bf16[512,256]{1,0:T(8,128)(2,1)S(1)}, bf16[224,256]{1,0:T(8,128)(2,1)S(1)}, bf16[224,256]{1,0:T(8,128)(2,1)S(1)}, bf16[256,512]{1,0:T(8,128)(2,1)S(1)}) custom-call(bf16[1,192,8192]{2,1,0:T(8,128)(2,1)} %anchor.1, bf16[1,192,3584]{2,1,0:T(8,128)(2,1)} %augment.1, s32[1]{0:T(128)S(6)} %copy.13.lag_in, ...), custom_call_target="tpu_custom_call" | custom-call | tf_op jit(solution)/shard_map/block/pallas_call | solution.py:675
  102.3 1.0 hand_on.1

commit v4 on v3

--- a/solution.py
+++ b/solution.py
@@ -14,21 +14,21 @@
 NS = 8
 COPIES = 256
 
-Q_Y, O_Y, GQ_Y, GO_Y = 416, 96, 416, 128
-
-FIRST = ('kv', 'qA', 'qB')
-O_LAST_Y = 1
+Q_Y, O_Y, GQ_Y, GO_Y = 320, 128, 192, 96
+
+FIRST = ('kv', 'qB', 'qA')
+O_LAST_Y = 0
 
 ORDER = (
-    "z1a", "z1b", "kv.fx", "kv.fy", "qA.fx", "qB.fx", "z2a", "turn0", "turn1", "turn2", "turn3", "turn4",
-    "turn5", "qB.fy", "turn6", "z2b", "turn7", "kv.fxf", "z3a", "qA.fxf", "own_o", "qB.fxf", "z3b", "kv",
-    "z4a", "oB.fx", "oA.fx", "q", "oB.fy", "oA.fxf", "attn0", "attn1", "attn2", "oB.fxf", "goA.y0", "goA.y1",
-    "goA.y2", "goA.y3", "goB.a0", "goB.a1", "goB.b0", "goB.b1", "goA.m", "goB.m0", "bc", "upd", "goA.a",
-    "goB.p0", "goB.p1", "bwd0", "bwd1", "bwd2", "goA.b", "goA.b_", "goA.p", "goA.p_", "u2a", "goB.y",
-    "gkv.a0", "gkv.a1", "gqA.y0", "gqA.y1", "gqA.y2", "gqA.y3", "gkv.b0", "gkv.b1", "u3b", "gqB.a0", "gqB.a1",
-    "gqB.b0", "gqB.b1", "gkv.m0", "gqA.m", "goA.f", "goB.f", "gqB.m0", "gkv.p0", "u3a", "gkv.p1", "gqA.a",
-    "u4b", "gqB.p0", "gqA.b", "gqB.p1", "u4a", "gqA.b_", "gkv.y", "gqA.p", "gqA.p_", "u5", "gqB.y", "gkv.f",
-    "gqA.f", "ufin", "gqB.f",
+    "z1a", "z1b", "kv.fx", "qB.fx", "kv.fy", "qA.fx", "z2a", "qB.fy", "turn0", "turn1", "turn2", "turn3",
+    "turn4", "turn5", "q0", "z2b", "turn6", "turn7", "e0", "kv.fxf", "z3a", "own_o", "qA.fxf", "qB.fxf",
+    "z3b", "e1", "kv", "z4a", "oA.fx", "oB.fy", "oB.fx", "q", "oA.fxf", "e2", "attn0", "oB.fxf", "attn1",
+    "attn2", "e3", "goB.a0", "goB.a1", "goB.b0", "upd", "upd2", "goB.b1", "goA.y0", "goA.y1", "goA.y2",
+    "goA.y3", "bc", "e4", "goB.m0", "goA.m", "goB.p0", "goB.p1", "bwd0", "u2a", "bwd1", "bwd2", "goA.a",
+    "goA.b", "u3b", "goA.b_", "goB.y", "gqB.a0", "gqB.a1", "gqB.b0", "gqB.b1", "goA.p", "goA.p_", "gqA.y0",
+    "gqA.y1", "gqA.y2", "gqA.y3", "gqB.m0", "gqA.m", "u3a", "kvf", "gqB.p0", "gqB.p1", "gkv.a", "gkv.b",
+    "goB.f", "gkv.m", "u4b", "gqA.a", "goA.f", "gqA.b", "u4a", "gqA.b_", "gqB.y", "gkv.p", "u5", "gqA.p",
+    "gqA.p_", "gqB.f", "u6", "gkv.f", "gqA.f", "ufin",
 )
 
 
@@ -49,7 +49,7 @@
     update, g_query, g_key, g_value, g_out,
     anc, anc_t, sts, sts_t, cot, wq, wkv, wo,
     s_out, s_kv, s_q, upd, rz, ru,
-    ra_out, rc_out, ry_out, ra_kv, rc_kv, ry_kv, ra_q, rc_q, ry_q,
+    ra_out, rc_out, ry_out, ra_kv, rc_kv, sts_y, kvb_y, ra_q, rc_q, ry_q,
     part, part_kv, other, other_kv, q_h, k_h, v_h, b_h, probs, att, ctx, qb, kvb,
     lag, stage,
     send, recv, near_send, near_recv, fin_recv, local,
@@ -277,6 +277,25 @@
     for i in range(NS):
         tasks["turn%d" % i] = turn(i)
 
+    def states_y():
+        k = 2 * (z // 2) + 1 - dp % 2
+        src = sts_t.at[pl.ds(pl.multiple_of((2 * k + c) * 224 + (z % 2) * 112, 112), 112)]
+        push("E0", src, sts_y.at[pl.ds(pl.multiple_of(z * 112, 112), 112)], to_yp)
+
+    def states_ring(step):
+        def run():
+            wait("E%d" % (step - 1))
+            s = sts_y.at[pl.ds(pl.multiple_of(((z + 9 - step) % NS) * 112, 112), 112)]
+            push("E%d" % step, s, s, to_zr)
+            if step < 4:
+                s = sts_y.at[pl.ds(pl.multiple_of(((z + step - 1) % NS) * 112, 112), 112)]
+                push("E%d" % step, s, s, to_zl)
+        return run
+
+    tasks["e0"] = states_y
+    for step in range(1, 5):
+        tasks["e%d" % step] = states_ring(step)
+
     def keys_values():
         wait(*kv_all)
         part_kv[...] = nn(sts[:, pl.ds(0, 512)], wkv[pl.ds(0, 512), :])
@@ -289,15 +308,16 @@
         push("exk", part_kv.at[:, head_o], other_kv.at[0], to_sib)
         push("exk", part_kv.at[:, head_vo], other_kv.at[1], to_sib)
 
+    def queries_near():
+        wait("qAy", "qAr", "qAl", "qBy", "qBr", "qBl")
+        part[0] = nn(anc[dp], wq[dp])
+        for k in (yp, xl, xr):
+            part[0] += nn(anc[k], wq[k])
+
     def queries():
         wait(*q_all)
-        part[0] = nn(anc[0], wq[0])
-
-        def add_q(k, _):
+        for k in (flip(xl), flip(xr), far, flip(far)):
             part[0] += nn(anc[k], wq[k])
-            return _
-
-        lax.fori_loop(1, NS, add_q, 0)
         push("exq", part.at[0, :, head_o], other.at[0], to_sib)
 
     factor = HEAD ** (-0.5)
@@ -322,11 +342,11 @@
             a = p.astype(BF)
             att[rows, :] = a
             ctx[rows, head] = nn(a, v_h[...]).astype(BF)
-            if r == LEN // block - 1:
-                push("ectx", ctx.at[:, head], ctx.at[:, head], to_sib)
+            push("ectx%d" % r, ctx.at[rows, head], ctx.at[rows, head], to_sib)
         return run
 
     tasks["kv"] = keys_values
+    tasks["q0"] = queries_near
     tasks["q"] = queries
     for r in range(LEN // block):
         tasks["attn%d" % r] = attend(r)
@@ -366,6 +386,8 @@
             if r == LEN // block - 1:
                 kvb[:, head] = other_kv[0].astype(BF)
                 kvb[:, head_v] = other_kv[1].astype(BF)
+                push("KX", kvb.at[:, head], kvb_y.at[:, head], to_yp)
+                push("KX", kvb.at[:, head_v], kvb_y.at[:, head_v], to_yp)
                 push("ekb", kvb.at[:, head], kvb.at[:, head], to_sib)
                 push("ekb", kvb.at[:, head_v], kvb.at[:, head_v], to_sib)
                 push("ekb", qb.at[:, head], qb.at[:, head], to_sib)
@@ -373,6 +395,13 @@
 
     for r in range(LEN // block):
         tasks["bwd%d" % r] = backward(r)
+
+    def hand_over():
+        wait("KX")
+        push("KF", kvb_y.at[:, head], kvb_y.at[:, head], to_sib)
+        push("KF", kvb_y.at[:, head_v], kvb_y.at[:, head_v], to_sib)
+
+    tasks["kvf"] = hand_over
 
     def slot(off, j):
         k = (dp + 2 * off + NS) % NS
@@ -504,6 +533,45 @@
         tasks[name + ".p_"] = on_left
         tasks[name + ".f"] = finish
 
+    def sum_x(name, ready, s, n, ra, rc, make, out):
+        h = n // 2
+        lo, hi = pl.ds(0, h), pl.ds(h, h)
+
+        def first():
+            ready()
+            k = slot(2, 0)
+            make(k, 0, n)
+            push(name + "a", s.at[k, lo], ra.at[0], to_xr)
+            push(name + "a", s.at[k, hi], ra.at[1], to_xl)
+
+        def second():
+            k, m = slot(1, 0), slot(-1, 0)
+            make(k, 0, n)
+            push(name + "b", s.at[k, hi], rc.at[0, hi], to_xr)
+            make(m, 0, n)
+            push(name + "b", s.at[m, lo], rc.at[1, lo], to_xl)
+
+        def own():
+            make(slot(0, 0), 0, n)
+
+        def on():
+            wait(name + "a")
+            k, m = slot(1, 0), slot(-1, 0)
+            add(s, k, lo, ra[0])
+            push(name + "p", s.at[k, lo], rc.at[0, lo], to_xr)
+            add(s, m, hi, ra[1])
+            push(name + "p", s.at[m, hi], rc.at[1, hi], to_xl)
+
+        def finish():
+            wait(name + "b", name + "p")
+            out(s[slot(0, 0)].astype(F32) + rc[0].astype(F32) + rc[1].astype(F32), 0, n)
+
+        tasks[name + ".a"] = first
+        tasks[name + ".b"] = second
+        tasks[name + ".m"] = own
+        tasks[name + ".p"] = on
+        tasks[name + ".f"] = finish
+
     def make_out(k, r0, n):
         s_out[k, pl.ds(r0, n)] = tn(ctx[:, pl.ds(r0, n)], cot[k]).astype(BF)
 
@@ -511,7 +579,8 @@
         g_out[pl.ds(r0, n)] = total.astype(BF)
 
     def make_kv(k, r0, n):
-        s_kv[k] = nn(sts_t[pl.ds(pl.multiple_of((2 * k + c) * 224, 224), 224), :], kvb[...]).astype(BF)
+        own_ = nn(sts_t[pl.ds(pl.multiple_of((2 * k + c) * 224, 224), 224), :], kvb[...])
+        s_kv[k] = (own_ + nn(sts_y[pl.ds(pl.multiple_of((k // 2) * 224, 224), 224), :], kvb_y[...])).astype(BF)
 
     def put_kv(total, r0, n):
         g_key[...] = total[:, :256].astype(BF)
@@ -523,12 +592,17 @@
     def put_q(total, r0, n):
         g_query[pl.ds(r0, n)] = total.astype(BF)
 
+    ctx_all = ["ectx%d" % r for r in range(LEN // block)]
+
     def ctx_ready():
         wait(*z_all)
-        wait("ectx")
+        wait(*ctx_all)
 
     def back_ready():
         wait("ekb")
+
+    def both_ready():
+        wait("ekb", "KF", "E1", "E2", "E3", "E4")
 
     ra_oa, ra_ob = ra_out
     rc_oa, rc_ob = rc_out
@@ -540,7 +614,7 @@
         sum_y_first("goA", ctx_ready, s_out, 0, GO_Y, ra_oa, rc_oa, ry_oa, make_out, put_out)
     if GO_Y < 256:
         sum_x_first("goB", ctx_ready, s_out, GO_Y, 256 - GO_Y, ra_ob, rc_ob, ry_ob, make_out, put_out)
-    sum_x_first("gkv", back_ready, s_kv, 0, 224, ra_kv, rc_kv, ry_kv, make_kv, put_kv)
+    sum_x("gkv", both_ready, s_kv, 224, ra_kv, rc_kv, make_kv, put_kv)
     if GQ_Y:
         sum_y_first("gqA", back_ready, s_q, 0, GQ_Y, ra_qa, rc_qa, ry_qa, make_q, put_q)
     if GQ_Y < 512:
@@ -553,64 +627,93 @@
             if step > 1 and (step, part_) != (2, "b"):
                 wait("U%d%s" % (step - 1, part_))
                 add(upd, k, a, rz[0, step - 2, a])
-                push("U%d%s" % (step, part_), upd.at[k, a], rz.at[0, step - 1, a], to_zr)
                 add(upd, m, b, rz[1, step - 2, b])
-                push("U%d%s" % (step, part_), upd.at[m, b], rz.at[1, step - 1, b], to_zl)
+            if (step, part_) == (4, "a"):
+                for i, name in enumerate(("U4a", "U4c")):
+                    first_, second_ = pl.ds(i * 96, 96), pl.ds(TOK + i * 96, 96)
+                    push(name, upd.at[k, first_], rz.at[0, 3, first_], to_zr)
+                    push(name, upd.at[m, second_], rz.at[1, 3, second_], to_zl)
             else:
                 push("U%d%s" % (step, part_), upd.at[k, a], rz.at[0, step - 1, a], to_zr)
                 push("U%d%s" % (step, part_), upd.at[m, b], rz.at[1, step - 1, b], to_zl)
         return run
 
-    def updates():
-        wait("ectx")
+    def make_upd(off):
+        k = (z + off) % NS
+        upd[k] = nn(ctx[...], wo[k]).astype(BF)
+
+    def updates_far():
+        wait(*ctx_all)
         wait(*o_all)
-
-        def make_upd(k, _):
-            upd[k] = nn(ctx[...], wo[k]).astype(BF)
-            return _
-
-        lax.fori_loop(0, NS, make_upd, 0)
+        for off in (4, 3, 5):
+            make_upd(off)
         ring_add(1, "a")()
         ring_add(2, "b")()
 
-    tasks["upd"] = updates
+    def updates():
+        for off in (2, 6, 1, 7, 0):
+            make_upd(off)
+
+    tasks["upd"] = updates_far
+    tasks["upd2"] = updates
     for step in (2, 3, 4):
         for part_ in ("a", "b"):
             if (step, part_) != (2, "b"):
                 tasks["u%d%s" % (step, part_)] = ring_add(step, part_)
 
-    given = upd.at[z, pl.ds(pl.multiple_of(o * TOK, TOK), TOK)]
-    fin_own = pltpu.make_async_copy(upd.at[z, mine], ru.at[0], fin_recv.at[0])
-    fin_sib = pltpu.make_async_remote_copy(
-        src_ref=given, dst_ref=ru.at[0], send_sem=near_send.at[2], recv_sem=fin_recv.at[0],
-        device_id=to_sib, device_id_type=MESH)
-    fin_far = [
-        pltpu.make_async_remote_copy(
-            src_ref=upd.at[z, pl.ds(h * TOK, TOK)], dst_ref=ru.at[1], send_sem=near_send.at[3 + h],
-            recv_sem=fin_recv.at[1], device_id=(dp, h, ty), device_id_type=MESH)
-        for h in (0, 1)
-    ]
-
-    def last_exchange():
-        wait("U4a", "U4b")
-        upd[z] = (upd[z].astype(F32) + rz[0, 3].astype(F32) + rz[1, 3].astype(F32)).astype(BF)
-
-        @pl.when(same)
-        def _():
-            fin_own.start()
-            fin_sib.start()
-
-        @pl.when(jnp.logical_not(same))
-        def _():
-            fin_far[0].start()
-            fin_far[1].start()
+    def last_copies(i):
+        rows = pl.ds(i * 96, 96)
+
+        def half(h):
+            return upd.at[z, pl.ds(pl.multiple_of(h * TOK + i * 96, 96), 96)]
+
+        own_ = pltpu.make_async_copy(half(c), ru.at[0, rows], fin_recv.at[2 * i])
+        sib_ = pltpu.make_async_remote_copy(
+            src_ref=half(o), dst_ref=ru.at[0, rows], send_sem=near_send.at[2 + 3 * i], recv_sem=fin_recv.at[2 * i],
+            device_id=to_sib, device_id_type=MESH)
+        far_ = [
+            pltpu.make_async_remote_copy(
+                src_ref=half(h), dst_ref=ru.at[1, rows], send_sem=near_send.at[3 + 3 * i + h],
+                recv_sem=fin_recv.at[2 * i + 1], device_id=(dp, h, ty), device_id_type=MESH)
+            for h in (0, 1)
+        ]
+        return own_, sib_, far_
+
+    last = [last_copies(i) for i in (0, 1)]
+
+    def last_exchange(i):
+        def run():
+            if i == 0:
+                wait("U4a", "U4b")
+            else:
+                wait("U4c")
+            for h in (0, 1):
+                rows = pl.ds(h * TOK + i * 96, 96)
+                upd[z, rows] = (
+                    upd[z, rows].astype(F32) + rz[0, 3, rows].astype(F32) + rz[1, 3, rows].astype(F32)
+                ).astype(BF)
+            own_, sib_, far_ = last[i]
+
+            @pl.when(same)
+            def _():
+                own_.start()
+                sib_.start()
+
+            @pl.when(jnp.logical_not(same))
+            def _():
+                far_[0].start()
+                far_[1].start()
+        return run
 
     def last_sum():
         for i in (0, 1):
-            pltpu.make_async_copy(ru.at[i], ru.at[i], fin_recv.at[i]).wait()
+            rows = pl.ds(i * 96, 96)
+            for j in (0, 1):
+                pltpu.make_async_copy(ru.at[j, rows], ru.at[j, rows], fin_recv.at[2 * i + j]).wait()
         update[0] = (ru[0].astype(F32) + ru[1].astype(F32)).astype(BF)
 
-    tasks["u5"] = last_exchange
+    tasks["u5"] = last_exchange(0)
+    tasks["u6"] = last_exchange(1)
     tasks["ufin"] = last_sum
 
     for name in ORDER:
@@ -624,12 +727,14 @@
     @pl.when(jnp.logical_not(same))
     def _():
         cot_sib.wait_send()
-        fin_far[0].wait_send()
-        fin_far[1].wait_send()
+        for _, _, far_ in last:
+            far_[0].wait_send()
+            far_[1].wait_send()
 
     @pl.when(same)
     def _():
-        fin_sib.wait_send()
+        for _, sib_, _ in last:
+            sib_.wait_send()
 
 
 def hand_on(*refs):
@@ -659,14 +764,14 @@
         vm((NS, 256, 512), BF), vm((NS, 224, 512), BF), vm((NS, 512, 256), BF),
         vm((NS, LEN, 512), BF), vm((2, 4, LEN, 512), BF), vm((2, TOK, 512), BF),
         *landing(256, 512, GO_Y),
-        vm((2, 2, 112, 512), BF), vm((2, 2, 224, 512), BF), vm((224, 512), BF),
+        vm((2, 112, 512), BF), vm((2, 224, 512), BF), vm((896, LEN), BF), vm((LEN, 512), BF),
         *landing(512, 256, GQ_Y),
         vm((2, LEN, 256), F32), vm((LEN, 512), F32), vm((2, LEN, HEAD), F32), vm((2, LEN, HEAD), F32),
         vm((LEN, HEAD), BF), vm((LEN, HEAD), BF), vm((LEN, HEAD), BF), vm((LEN, HEAD), BF),
         vm((LEN, LEN), F32), vm((LEN, LEN), BF), vm((LEN, 256), BF), vm((LEN, 256), BF), vm((LEN, 512), BF),
         pltpu.SMEM((1,), jnp.int32), vm((TOK, 512), BF),
         pltpu.SemaphoreType.DMA((COPIES,)), pltpu.SemaphoreType.DMA((COPIES,)),
-        pltpu.SemaphoreType.DMA((5,)), pltpu.SemaphoreType.DMA((2,)), pltpu.SemaphoreType.DMA((2,)),
+        pltpu.SemaphoreType.DMA((8,)), pltpu.SemaphoreType.DMA((2,)), pltpu.SemaphoreType.DMA((4,)),
         pltpu.SemaphoreType.DMA((16,)),
     ]
     any_ = pl.BlockSpec(memory_space=pl.ANY)

time: 103 us -> 99.8 us (0.969)
  Pallas kernels: 102 us -> 98.2 us
    pallas_call x1, Pallas kernels: 101 us -> 97.2 us  [local(): pl.pallas_call(kernel, out_shape=[pltpu.VMEM(s, d) for s, d in shapes], i...]
where the time goes in v4:
time: 99.8 us; the launch traced here: 99.7 us
  Pallas kernels  98.2 us (98%)
  between operations  1.45 us (1%)
    pallas_call x1, Pallas kernels, local(): pl.pallas_call(kernel, out_shape=[pltpu.VMEM(s, d) for s, d in shapes], i...  97.2 us

profile of v4, /device:TPU:1, one launch (start us, length us, event | category | flops | bytes accessed | tf_op | source)
XLA Modules:
  0.0 99.7 jit_solution(4097917841526998324)
XLA Ops:
  1.3 97.2 %block.1 = (bf16[1,192,512]{2,1,0:T(8,128)(2,1)S(1)}, bf16[512,256]{1,0:T(8,128)(2,1)S(1)}, bf16[224,256]{1,0:T(8,128)(2,1)S(1)}, bf16[224,256]{1,0:T(8,128)(2,1)S(1)}, bf16[256,512]{1,0:T(8,128)(2,1)S(1)}) custom-call(bf16[1,192,8192]{2,1,0:T(8,128)(2,1)} %anchor.1, bf16[1,192,3584]{2,1,0:T(8,128)(2,1)} %augment.1, s32[1]{0:T(128)S(6)} %copy.13.lag_in, ...), custom_call_target="tpu_custom_call" | custom-call | tf_op jit(solution)/shard_map/block/pallas_call | solution.py:780
  98.5 1.0 hand_on.1

commit v5 on v4

--- a/solution.py
+++ b/solution.py
@@ -14,21 +14,16 @@
 NS = 8
 COPIES = 256
 
-Q_Y, O_Y, GQ_Y, GO_Y = 320, 128, 192, 96
+Q_Y, O_Y, GQ_Y, GO_Y = 288, 128, 256, 96
 
 FIRST = ('kv', 'qB', 'qA')
-O_LAST_Y = 0
+O_LAST_Y = bool(0)
 
 ORDER = (
-    "z1a", "z1b", "kv.fx", "qB.fx", "kv.fy", "qA.fx", "z2a", "qB.fy", "turn0", "turn1", "turn2", "turn3",
-    "turn4", "turn5", "q0", "z2b", "turn6", "turn7", "e0", "kv.fxf", "z3a", "own_o", "qA.fxf", "qB.fxf",
-    "z3b", "e1", "kv", "z4a", "oA.fx", "oB.fy", "oB.fx", "q", "oA.fxf", "e2", "attn0", "oB.fxf", "attn1",
-    "attn2", "e3", "goB.a0", "goB.a1", "goB.b0", "upd", "upd2", "goB.b1", "goA.y0", "goA.y1", "goA.y2",
-    "goA.y3", "bc", "e4", "goB.m0", "goA.m", "goB.p0", "goB.p1", "bwd0", "u2a", "bwd1", "bwd2", "goA.a",
-    "goA.b", "u3b", "goA.b_", "goB.y", "gqB.a0", "gqB.a1", "gqB.b0", "gqB.b1", "goA.p", "goA.p_", "gqA.y0",
-    "gqA.y1", "gqA.y2", "gqA.y3", "gqB.m0", "gqA.m", "u3a", "kvf", "gqB.p0", "gqB.p1", "gkv.a", "gkv.b",
-    "goB.f", "gkv.m", "u4b", "gqA.a", "goA.f", "gqA.b", "u4a", "gqA.b_", "gqB.y", "gkv.p", "u5", "gqA.p",
-    "gqA.p_", "gqB.f", "u6", "gkv.f", "gqA.f", "ufin",
+    14, 15, 1, 21, 6, 22, 23, 24, 0, 25, 26, 3, 27, 16, 28, 5, 29, 35, 17, 2, 18, 13, 4, 30, 7, 19, 34, 20, 8,
+    10, 31, 11, 36, 9, 37, 38, 12, 39, 32, 56, 59, 57, 60, 45, 90, 91, 40, 46, 47, 48, 33, 62, 49, 58, 50, 41,
+    61, 42, 92, 43, 51, 52, 94, 53, 54, 70, 71, 72, 73, 63, 81, 84, 82, 85, 74, 87, 55, 44, 83, 93, 86, 65,
+    66, 75, 67, 96, 76, 88, 77, 95, 68, 78, 79, 64, 97, 98, 89, 69, 80, 99,
 )
 
 
@@ -139,9 +134,12 @@
         tasks[name + ".fy"] = from_y
         tasks[name + ".fx"] = near("", "h", xl, xr)
         tasks[name + ".fxf"] = near("f", "g", flip(xl), flip(xr))
-        push(name + "y", mine_, mine_, to_yp)
-        push(name + "r", mine_, mine_, to_xr)
-        push(name + "l", mine_, mine_, to_xl)
+        def start():
+            push(name + "y", mine_, mine_, to_yp)
+            push(name + "r", mine_, mine_, to_xr)
+            push(name + "l", mine_, mine_, to_xl)
+
+        starts[name] = start
         return [name + e for e in ("y", "r", "l", "fr", "fl", "h0", "h1", "g0", "g1")]
 
     def x_first(name, slot, r0, n):
@@ -165,9 +163,12 @@
 
         tasks[name + ".fx"] = from_x
         tasks[name + ".fxf"] = from_far
-        push(name + "r", mine_, mine_, to_xr)
-        push(name + "l", mine_, mine_, to_xl)
-        push(name + "y", mine_, mine_, to_yp)
+        def start():
+            push(name + "r", mine_, mine_, to_xr)
+            push(name + "l", mine_, mine_, to_xl)
+            push(name + "y", mine_, mine_, to_yp)
+
+        starts[name] = start
         return [name + e for e in ("y", "r", "l", "h0", "h1", "y0", "y1", "g0", "g1")]
 
     own_kv = kv_rows(dp, 0, 224)
@@ -178,8 +179,7 @@
     fetch(w_out, wo.at[dp])
     early = len(locals_)
     fetch(lag_in, lag)
-    for copy in locals_[:early]:
-        copy.wait()
+    locals_[0].wait()
     pl.semaphore_wait(barrier, len(partners))
 
     cot_dst = cot.at[z, mine]
@@ -200,34 +200,26 @@
     def _():
         cot_sib.start()
 
-    kv_all, q_all, o_all = [], [], []
-
-    def gather_q_a():
-        if Q_Y:
-            q_all.extend(x_first("qA", rows_of(wq), 0, Q_Y))
-
-    def gather_q_b():
-        if Q_Y < 512:
-            q_all.extend(y_first("qB", rows_of(wq), Q_Y, 512 - Q_Y))
-
-    def gather_kv():
-        kv_all.extend(y_first("kv", slot_kv, 0, 224))
-
-    first = {"kv": gather_kv, "qA": gather_q_a, "qB": gather_q_b}
+    starts = {}
+    kv_all = y_first("kv", slot_kv, 0, 224)
+    q_all, o_all = [], []
+    if Q_Y:
+        q_all += x_first("qA", rows_of(wq), 0, Q_Y)
+    if Q_Y < 512:
+        q_all += y_first("qB", rows_of(wq), Q_Y, 512 - Q_Y)
+    if O_Y:
+        o_all += x_first("oA", rows_of(wo), 0, O_Y)
+    if O_Y < 256:
+        o_all += y_first("oB", rows_of(wo), O_Y, 256 - O_Y)
+    for copy in locals_[1:4]:
+        copy.wait()
     for name in FIRST:
-        first[name]()
-
-    def gather_o_a():
-        if O_Y:
-            o_all.extend(x_first("oA", rows_of(wo), 0, O_Y))
-
-    def gather_o_b():
-        if O_Y < 256:
-            o_all.extend(y_first("oB", rows_of(wo), O_Y, 256 - O_Y))
+        starts.pop(name)()
 
     def own_o():
-        for run in (gather_o_b, gather_o_a) if O_LAST_Y else (gather_o_a, gather_o_b):
-            run()
+        locals_[4].wait()
+        for name in sorted(starts, reverse=O_LAST_Y):
+            starts[name]()
 
     tasks["own_o"] = own_o
 
@@ -716,9 +708,11 @@
     tasks["u6"] = last_exchange(1)
     tasks["ufin"] = last_sum
 
-    for name in ORDER:
-        tasks.pop(name)()
-    assert not tasks and not arriving
+    steps = list(tasks.values())
+    assert sorted(ORDER) == list(range(len(steps)))
+    for i in ORDER:
+        steps[i]()
+    assert not arriving
 
     for copy in started:
         copy.wait_send()

time: 99.8 us -> 99.4 us (level)
  no operation moved by 1% of the time
where the time goes in v5:
time: 99.4 us; the launch traced here: 99.3 us
  Pallas kernels  97.9 us (98%)
  between operations  1.45 us (1%)
    pallas_call x1, Pallas kernels, local(): pl.pallas_call(kernel, out_shape=[pltpu.VMEM(s, d) for s, d in shapes], i...  96.9 us

profile of v5, /device:TPU:1, one launch (start us, length us, event | category | flops | bytes accessed | tf_op | source)
XLA Modules:
  0.0 99.3 jit_solution(13638561934598573487)
XLA Ops:
  1.3 96.9 %block.1 = (bf16[1,192,512]{2,1,0:T(8,128)(2,1)S(1)}, bf16[512,256]{1,0:T(8,128)(2,1)S(1)}, bf16[224,256]{1,0:T(8,128)(2,1)S(1)}, bf16[224,256]{1,0:T(8,128)(2,1)S(1)}, bf16[256,512]{1,0:T(8,128)(2,1)S(1)}) custom-call(bf16[1,192,8192]{2,1,0:T(8,128)(2,1)} %anchor.1, bf16[1,192,3584]{2,1,0:T(8,128)(2,1)} %augment.1, s32[1]{0:T(128)S(6)} %copy.13.lag_in, ...), custom_call_target="tpu_custom_call" | custom-call | tf_op jit(solution)/shard_map/block/pallas_call | solution.py:774
  98.2 1.0 hand_on.1

commit v6 on v5

--- a/solution.py
+++ b/solution.py
@@ -25,6 +25,9 @@
     61, 42, 92, 43, 51, 52, 94, 53, 54, 70, 71, 72, 73, 63, 81, 84, 82, 85, 74, 87, 55, 44, 83, 93, 86, 65,
     66, 75, 67, 96, 76, 88, 77, 95, 68, 78, 79, 64, 97, 98, 89, 69, 80, 99,
 )
+
+SWEEPS = (96,)
+EARLY = 130
 
 
 def nn(a, b):
@@ -710,11 +713,16 @@
 
     steps = list(tasks.values())
     assert sorted(ORDER) == list(range(len(steps)))
-    for i in ORDER:
+    gone = 0
+    for n, i in enumerate(ORDER):
+        if n in SWEEPS:
+            for copy in started[:EARLY]:
+                copy.wait_send()
+            gone = EARLY
         steps[i]()
     assert not arriving
 
-    for copy in started:
+    for copy in started[gone:]:
         copy.wait_send()
     cot_far.wait_send()
 

time: 99.4 us -> 99.2 us (level)
  no operation moved by 1% of the time
where the time goes in v6:
time: 99.2 us; the launch traced here: 99.1 us
  Pallas kernels  97.7 us (98%)
  between operations  1.45 us (1%)
    pallas_call x1, Pallas kernels, local(): pl.pallas_call(kernel, out_shape=[pltpu.VMEM(s, d) for s, d in shapes], i...  96.7 us

profile of v6, /device:TPU:1, one launch (start us, length us, event | category | flops | bytes accessed | tf_op | source)
XLA Modules:
  0.0 99.1 jit_solution(1809685802500149775)
XLA Ops:
  1.3 96.7 %block.1 = (bf16[1,192,512]{2,1,0:T(8,128)(2,1)S(1)}, bf16[512,256]{1,0:T(8,128)(2,1)S(1)}, bf16[224,256]{1,0:T(8,128)(2,1)S(1)}, bf16[224,256]{1,0:T(8,128)(2,1)S(1)}, bf16[256,512]{1,0:T(8,128)(2,1)S(1)}) custom-call(bf16[1,192,8192]{2,1,0:T(8,128)(2,1)} %anchor.1, bf16[1,192,3584]{2,1,0:T(8,128)(2,1)} %augment.1, s32[1]{0:T(128)S(6)} %copy.13.lag_in, ...), custom_call_target="tpu_custom_call" | custom-call | tf_op jit(solution)/shard_map/block/pallas_call | solution.py:782
  98.0 1.0 hand_on.1
